TPU v7x, 512 devices: a whole 4x4x16 slice. The times are simulated.
512 devices in a mesh: dp: 64 (over x, z), fsdp: 8 (over y, core).
Axes of the slice: x: 4, y: 4, z: 16, core: 2. Of those that a mesh axis runs over, the one named last changes fastest.
Arguments:
- actions: bfloat16 [8, 8192, 1024], P('fsdp', 'dp'), may hold values from -6 to 6
- lengths: int32 [8, 64, 7], P('fsdp', 'dp'), may hold values from 1 to 74, as said below
- partner_mask: int32 [8, 64], P('fsdp', 'dp'), may hold values from 1 to 7, as said below
- norm_gain: float32 [1024], replicated, may hold values from 0.1 to 1.9
- w_in: bfloat16 [1024, 4096], P('fsdp'), may hold values from -0.1875 to 0.1875
- w_out: bfloat16 [1024, 1024], P('fsdp'), may hold values from -0.1875 to 0.1875
- cotangent: bfloat16 [8, 8192, 1024], P('fsdp', 'dp'), may hold values from -16 to 16
Outputs:
- output: bfloat16 [8, 8192, 1024], P('fsdp', 'dp')
- grad_input: bfloat16 [8, 8192, 1024], P('fsdp', 'dp')
- grad_weights: float32 [1024, 1024], P('dp')
Inputs may be any that keep to these rules, and one draw needn't show every extreme that they name: The 7 lengths of each block sum to 80. partner_mask is equal over aligned groups of 8 indices of dp within a stream, so block b and block b XOR partner_mask[., b] name each other.
All inputs are finite; a program needn't handle non-finite values.
Results may differ from a plain program's by a relative error of at most 0.015.
Values may be sent and summed in bfloat16 or wider, within the bound.
A program may use at most 128 MiB of HBM per device.

v0:
```python
import jax
import jax.numpy as jnp
from jax import lax
from jax.sharding import PartitionSpec as P

HEADS = 8
HEAD_DIM = 128
SPILL = 16
MOST = 32


EPSILON = 1e-05


def swapped(array, axis, distance):
    return lax.ppermute(array, axis, [(i, i ^ 1 << distance) for i in range(lax.axis_size(axis))])


def silu_slope(values):
    sigma = jax.nn.sigmoid(values)
    return sigma * (1.0 + values * (1.0 - sigma))


def normalize(values):
    centred = values - jnp.mean(values, axis=-1, keepdims=True)
    inverse = lax.rsqrt(jnp.mean(centred * centred, axis=-1, keepdims=True) + EPSILON)
    return (centred * inverse, inverse)


def norm_backward(grad, normed, inverse):
    return inverse * (
        grad
        - jnp.mean(grad, axis=-1, keepdims=True)
        - normed * jnp.mean(grad * normed, axis=-1, keepdims=True)
    )


def user_starts(user_lengths, positions):
    ends = jnp.cumsum(user_lengths, dtype=jnp.int32)
    before = jnp.where(
        ends[None, :] <= positions[:, None], user_lengths[None, :], jnp.zeros((), jnp.int32)
    )
    return jnp.sum(before, axis=1, dtype=jnp.int32)


def route_partner(value, mask_bits, mover):
    for bit in range(3):
        moved = mover(value, bit)
        value = jnp.where(mask_bits >> bit & 1 == 1, moved, value)
    return value


def score_of(query_heads, key_heads):
    return jnp.einsum(
        "qhd,khd->hqk", query_heads, key_heads, preferred_element_type=jnp.float32
    ) * HEAD_DIM ** (-0.5)


def per_device(actions, lengths, partner_mask, norm_gain, w_in, w_out, cotangent):
    width = HEADS * HEAD_DIM
    rows = actions.shape[1]
    first = rows - SPILL - MOST
    spare_start = rows - SPILL
    back_scale = HEAD_DIM ** (-0.5) / MOST
    all_rows = rows * lax.axis_size("dp") * lax.axis_size("fsdp")
    mask_bits = partner_mask[0, 0]
    inputs = actions[0].astype(jnp.float32)
    incoming = cotangent[0]
    normed_in, inverse_in = normalize(inputs)
    normed = (normed_in * norm_gain).astype(jnp.bfloat16)
    in_whole = lax.all_gather(w_in, "fsdp", axis=0, tiled=True)
    hidden = jnp.dot(normed, in_whole, preferred_element_type=jnp.float32)
    out_whole = lax.all_gather(w_out, "fsdp", axis=0, tiled=True)
    active = jax.nn.silu(hidden).astype(jnp.bfloat16)
    gates = active[:, :width]
    value_heads = active[:, width : 2 * width].reshape(rows, HEADS, HEAD_DIM)
    query_heads = active[:, 2 * width : 3 * width].reshape(rows, HEADS, HEAD_DIM)
    key_heads = active[:, 3 * width :].reshape(rows, HEADS, HEAD_DIM)
    spare_queries = query_heads[spare_start:]
    positions = jnp.arange(rows, dtype=jnp.int32)
    all_lengths = jnp.concatenate([lengths[0, 0], jnp.array([MOST, SPILL], dtype=jnp.int32)])
    starts = user_starts(all_lengths, positions)
    visible = (positions[None, :] >= starts[:, None]) & (positions[None, :] <= positions[:, None])
    scores = score_of(query_heads, key_heads)
    weights = (jnp.where(visible[None], jax.nn.silu(scores), 0.0) / MOST).astype(jnp.bfloat16)
    attended_local = jnp.einsum(
        "hqk,khd->qhd", weights, value_heads, preferred_element_type=jnp.float32
    )
    sent = jnp.concatenate(
        [
            active[first : first + MOST, 3 * width :],
            active[first : first + MOST, width : 2 * width],
        ],
        axis=1,
    )
    arrived = route_partner(sent, mask_bits, lambda value, bit: swapped(value, "dp", bit))
    far_keys = arrived[:, :width].reshape(MOST, HEADS, HEAD_DIM)
    far_values = arrived[:, width:].reshape(MOST, HEADS, HEAD_DIM)
    far_scores = score_of(spare_queries, far_keys)
    far_weights = (jax.nn.silu(far_scores) / MOST).astype(jnp.bfloat16)
    far_part = jnp.einsum(
        "hqk,khd->qhd", far_weights, far_values, preferred_element_type=jnp.float32
    )
    attended = jnp.concatenate(
        [attended_local[:spare_start], attended_local[spare_start:] + far_part], axis=0
    ).reshape(rows, width)
    normed_out, inverse_out = normalize(attended)
    mixed = (normed_out * gates.astype(jnp.float32)).astype(jnp.bfloat16)
    output = (jnp.dot(mixed, out_whole, preferred_element_type=jnp.float32) + inputs).astype(
        jnp.bfloat16
    )
    grad_mixed = lax.dot_general(
        incoming, out_whole, (((1,), (1,)), ((), ())), preferred_element_type=jnp.float32
    )
    grad_gates = grad_mixed * normed_out
    grad_attended = norm_backward(
        grad_mixed * gates.astype(jnp.float32), normed_out, inverse_out
    ).astype(jnp.bfloat16)
    grad_heads = grad_attended.reshape(rows, HEADS, HEAD_DIM)
    grad_w = jnp.einsum("qhd,khd->hqk", grad_heads, value_heads, preferred_element_type=jnp.float32)
    grad_scores = (jnp.where(visible[None], grad_w * silu_slope(scores), 0.0) * back_scale).astype(
        jnp.bfloat16
    )
    grad_queries = jnp.einsum(
        "hqk,khd->qhd", grad_scores, key_heads, preferred_element_type=jnp.float32
    )
    grad_keys = jnp.einsum(
        "hqk,qhd->khd", grad_scores, query_heads, preferred_element_type=jnp.float32
    ).reshape(rows, width)
    grad_values = jnp.einsum(
        "hqk,qhd->khd", weights, grad_heads, preferred_element_type=jnp.float32
    ).reshape(rows, width)
    spare_grad = grad_heads[spare_start:]
    far_grad_w = jnp.einsum(
        "qhd,khd->hqk", spare_grad, far_values, preferred_element_type=jnp.float32
    )
    far_grad_scores = (far_grad_w * silu_slope(far_scores) * back_scale).astype(jnp.bfloat16)
    query_extra = jnp.einsum(
        "hqk,khd->qhd", far_grad_scores, far_keys, preferred_element_type=jnp.float32
    )
    key_back = jnp.einsum(
        "hqk,qhd->khd", far_grad_scores, spare_queries, preferred_element_type=jnp.float32
    ).reshape(MOST, width)
    value_back = jnp.einsum(
        "hqk,qhd->khd", far_weights, spare_grad, preferred_element_type=jnp.float32
    ).reshape(MOST, width)
    returned = route_partner(
        jnp.concatenate([key_back, value_back], axis=1),
        mask_bits,
        lambda value, bit: swapped(value.astype(jnp.bfloat16), "dp", bit).astype(value.dtype),
    )
    key_extra = returned[:, :width]
    value_extra = returned[:, width:]
    grad_queries = jnp.concatenate(
        [grad_queries[:spare_start], grad_queries[spare_start:] + query_extra], axis=0
    ).reshape(rows, width)
    grad_keys = jnp.concatenate(
        [grad_keys[:first], grad_keys[first : first + MOST] + key_extra, grad_keys[spare_start:]],
        axis=0,
    )
    grad_values = jnp.concatenate(
        [
            grad_values[:first],
            grad_values[first : first + MOST] + value_extra,
            grad_values[spare_start:],
        ],
        axis=0,
    )
    grad_active = jnp.concatenate([grad_gates, grad_values, grad_queries, grad_keys], axis=1)
    grad_hidden = (grad_active * silu_slope(hidden)).astype(jnp.bfloat16)
    grad_normed = lax.dot_general(
        grad_hidden, in_whole, (((1,), (1,)), ((), ())), preferred_element_type=jnp.float32
    )
    grad_input = incoming.astype(jnp.float32) + norm_backward(
        grad_normed * norm_gain, normed_in, inverse_in
    )
    summed = lax.psum_scatter(
        lax.dot_general(
            incoming, mixed, (((0,), (0,)), ((), ())), preferred_element_type=jnp.float32
        ),
        "dp",
        scatter_dimension=0,
        tiled=True,
    )
    weight_grads = lax.psum(summed.astype(jnp.bfloat16), "fsdp").astype(jnp.float32) * all_rows ** (
        -0.5
    )
    return (output[None], grad_input.astype(jnp.bfloat16)[None], weight_grads)


def solution(mesh):
    placed = (
        P("fsdp", "dp", None),
        P("fsdp", "dp", None),
        P("fsdp", "dp"),
        P(),
        P("fsdp", None),
        P("fsdp", None),
        P("fsdp", "dp", None),
    )
    return jax.shard_map(
        per_device,
        mesh=mesh,
        in_specs=placed,
        out_specs=(P("fsdp", "dp", None), P("fsdp", "dp", None), P("dp", None)),
        check_vma=False,
    )
```

profile of v0, /device:TPU:1, one launch (start us, length us, event | category | flops | bytes accessed | tf_op | source)
XLA Modules:
  0.0 859.4 jit_solution(16114527493188560633)
XLA Ops:
  7.2 0.7 all-gather.3.cloned.1.call-update
  7.9 0.7 all-gather.5.cloned.1.call-update
  9.3 1.1 convert_reduce_fusion
  10.4 1.2 fusion.24
  11.6 0.8 fusion.76
  12.7 60.6 %all-gather.3.cloned.1.call-done = bf16[1024,4096]{1,0:T(8,128)(2,1)} async-done(((bf16[128,4096]{1,0:T(8,128)(2,1)}), bf16[1024,4096]{1,0:T(8,128)(2,1)}) %all-gather.3.cloned.1.call-update) | async-done | bytes 8388624 | tf_op jit(solution)/shard_map/all_gather | solution.py:71
  73.3 6.3 multiply_convert_fusion
  79.6 3.2 collective-permute-start
  82.9 3.5 collective-permute-done
  86.4 4.2 collective-permute-start.1
  90.6 0.3 convolution_multiply_fusion.2
  90.9 5.5 collective-permute-done.1
  96.4 7.4 collective-permute-start.2
  104.1 10.1 %collective-permute-done.2 = bf16[32,2048]{1,0:T(8,128)(2,1)S(1)} collective-permute-done((bf16[32,2048]{1,0:T(8,128)(2,1)S(1)}, bf16[32,2048]{1,0:T(8,128)(2,1)S(1)}, u32[]{:S(2)}, u32[]{:S(2)}) %collective-permute-start.2) | collective-permute-done | bytes 131104 | tf_op jit(solution)/shard_map/ppermute | solution.py:16
  114.9 2.8 convolution_bitcast_fusion
  117.7 5.3 copy.100
  123.1 2.5 fusion.55
  126.6 1.9 collective-permute-start.3
  128.5 0.3 convolution_bitcast_fusion.4
  128.9 0.4 fusion.3
  129.9 1.4 copy-done
  131.3 1.2 fusion.5
  132.7 4.5 collective-permute-start.4
  137.2 5.7 collective-permute-done.4
  143.0 9.2 %collective-permute-start.5 = (bf16[32,2048]{1,0:T(8,128)(2,1)S(1)}, bf16[32,2048]{1,0:T(8,128)(2,1)S(1)}, u32[]{:S(2)}, u32[]{:S(2)}) collective-permute-start(bf16[32,2048]{1,0:T(8,128)(2,1)S(1)} %fusion.56), channel_id=1, source_target_pairs={{0,32},{8,40},{16,48},{24,56},{32,0},{40,8},{48,16},{56,24},{64,96... | collective-permute-start | bytes 393224 | tf_op jit(solution)/shard_map/ppermute | solution.py:16
  152.3 11.9 %collective-permute-done.5 = bf16[32,2048]{1,0:T(8,128)(2,1)S(1)} collective-permute-done((bf16[32,2048]{1,0:T(8,128)(2,1)S(1)}, bf16[32,2048]{1,0:T(8,128)(2,1)S(1)}, u32[]{:S(2)}, u32[]{:S(2)}) %collective-permute-start.5) | collective-permute-done | bytes 131104 | tf_op jit(solution)/shard_map/ppermute | solution.py:16
  164.4 3.1 fusion.82
  167.4 1.0 fusion.29
  168.4 648.0 %reduce-scatter.4.cloned.1.call-done = f32[16,1024]{1,0:T(8,128)} async-done(((f32[1024,1024]{1,0:T(8,128)}), f32[16,1024]{1,0:T(8,128)}) %reduce-scatter.4.cloned.1.call-update) | async-done | bytes 65552
  816.5 1.0 copy.101
  817.5 34.5 %psum.7 = bf16[16,1024]{0,1:T(8,128)(2,1)S(1)} all-reduce(bf16[16,1024]{0,1:T(8,128)(2,1)S(1)} %copy.101), channel_id=1, replica_groups=mesh['dp'=64,'fsdp'=8] {'fsdp'}, use_global_device_ids=true, to_apply=%region_11.12 | all-reduce | flops 16384 | bytes 65536 | tf_op jit(solution)/shard_map/psum | solution.py:185
  852.0 0.8 copy.97
  (64 shorter events, 3.5 us)
Async XLA Ops:
  7.2 66.2 %all-gather.3.cloned.1.call-start = ((), (), s32[]{:S(2)}) async-start(), calls=%async_computation.1 | async-start | bytes 9437184 | tf_op jit(solution)/shard_map/all_gather | solution.py:71
  7.9 115.2 %all-gather.5.cloned.1.call-start = ((), (), s32[]{:S(2)}) async-start(), calls=%async_computation.2 | async-start | bytes 2359296 | tf_op jit(solution)/shard_map/all_gather | solution.py:73
  8.6 807.8 %reduce-scatter.4.cloned.1.call-start = ((), (), s32[]{:S(2)}) async-start(), calls=%async_computation.3 | async-start | bytes 4259840
  79.6 6.7 collective-permute-start
  86.4 10.0 %collective-permute-start.1 = (bf16[32,2048]{1,0:T(8,128)(2,1)S(1)}, bf16[32,2048]{1,0:T(8,128)(2,1)S(1)}, u32[]{:S(2)}, u32[]{:S(2)}) collective-permute-start(bf16[32,2048]{1,0:T(8,128)(2,1)S(1)} %broadcast_select_fusion), channel_id=1, source_target_pairs={{0,16},{8,24},{16,0},{24,8},{32,48},{40,56},{48,32},{56,40},{64,80... | collective-permute-start | bytes 393224 | tf_op jit(solution)/shard_map/ppermute | solution.py:16
  96.4 17.8 %collective-permute-start.2 = (bf16[32,2048]{1,0:T(8,128)(2,1)S(1)}, bf16[32,2048]{1,0:T(8,128)(2,1)S(1)}, u32[]{:S(2)}, u32[]{:S(2)}) collective-permute-start(bf16[32,2048]{1,0:T(8,128)(2,1)S(1)} %broadcast_select_fusion.1), channel_id=1, source_target_pairs={{0,32},{8,40},{16,48},{24,56},{32,0},{40,8},{48,16},{56,24},{64,96... | collective-permute-start | bytes 393224 | tf_op jit(solution)/shard_map/ppermute | solution.py:16
  104.1 10.8 %copy-start.2 = (bf16[1,128,1024]{2,1,0:T(8,128)(2,1)S(1)}, bf16[1,128,1024]{2,1,0:T(8,128)(2,1)}, u32[]{:S(2)}) copy-start(bf16[1,128,1024]{2,1,0:T(8,128)(2,1)} %param.14) | copy-start | bytes 786436
  126.6 6.0 collective-permute-start.3
  128.5 35.8 %slice-start = ((s8[8388608]{0:T(1024)(128)(4,1)}), s8[4194304]{0:T(1024)(128)(4,1)S(1)}, s32[]{:S(2)}) async-start(s8[8388608]{0:T(1024)(128)(4,1)} %bitcast.214), calls=%async_computation.4 | async-start | bytes 8388608
  129.3 2.0 copy-start
  129.3 2.0 copy-start.1
  129.6 34.7 %slice-start.1 = ((s8[8388608]{0:T(1024)(128)(4,1)}), s8[4194304]{0:T(1024)(128)(4,1)S(1)}, s32[]{:S(2)}) async-start(s8[8388608]{0:T(1024)(128)(4,1)} %bitcast.214), calls=%async_computation.5 | async-start | bytes 8388608
  132.7 10.3 %collective-permute-start.4 = (bf16[32,2048]{1,0:T(8,128)(2,1)S(1)}, bf16[32,2048]{1,0:T(8,128)(2,1)S(1)}, u32[]{:S(2)}, u32[]{:S(2)}) collective-permute-start(bf16[32,2048]{1,0:T(8,128)(2,1)S(1)} %fusion.54), channel_id=1, source_target_pairs={{0,16},{8,24},{16,0},{24,8},{32,48},{40,56},{48,32},{56,40},{64,80... | collective-permute-start | bytes 393224 | tf_op jit(solution)/shard_map/ppermute | solution.py:16
  137.2 27.1 %copy-start.3 = (f32[1024]{0:T(1024)S(1)}, f32[1024]{0:T(1024)}, u32[]{:S(2)}) copy-start(f32[1024]{0:T(1024)} %param.11) | copy-start | bytes 12292
  137.2 27.1 %copy-start.4 = (f32[128,4096]{1,0:T(8,128)S(1)}, f32[128,4096]{1,0:T(8,128)}, u32[]{:S(2)}) copy-start(f32[128,4096]{1,0:T(8,128)} %get-tuple-element.32) | copy-start | bytes 6291460
  143.0 21.2 %collective-permute-start.5 = (bf16[32,2048]{1,0:T(8,128)(2,1)S(1)}, bf16[32,2048]{1,0:T(8,128)(2,1)S(1)}, u32[]{:S(2)}, u32[]{:S(2)}) collective-permute-start(bf16[32,2048]{1,0:T(8,128)(2,1)S(1)} %fusion.56), channel_id=1, source_target_pairs={{0,32},{8,40},{16,48},{24,56},{32,0},{40,8},{48,16},{56,24},{64,96... | collective-permute-start | bytes 393224 | tf_op jit(solution)/shard_map/ppermute | solution.py:16
Sparse Core Ops, SparseCore 0:
  10.2 63.1 all-gather.2
  75.5 33.0 all-gather.4
  123.2 693.2 reduce-scatter.3
where the time goes:
time: 861 us; the launch traced here: 859 us
  waiting for transfers between devices  747 us (87%)
  blocking collectives  34.5 us (4%)
  starting transfers between devices  30.5 us (4%)
  matrix products  18.8 us (2%)
  between operations  14.8 us (2%)
  local copies, waits for them, and re-layouts  8.81 us (1%)
    unnamed x4, waiting for transfers between devices  649 us
    all_gather x1, waiting for transfers between devices, per_device(): in_whole = lax.all_gather(w_in, 'fsdp', axis=0, tiled=True)  60.6 us
    ppermute x6, waiting for transfers between devices, swapped(): lax.ppermute(array, axis, [(i, i ^ 1 << distance) for i in range(lax.axis...  36.6 us
    psum x1, blocking collectives, per_device(): lax.psum(summed.astype(jnp.bfloat16), 'fsdp').astype(jnp.float32)  34.5 us
    ppermute x6, starting transfers between devices, swapped(): lax.ppermute(array, axis, [(i, i ^ 1 << distance) for i in range(lax.axis...  30.4 us
  transfers between devices with their start and end apart: 9, of which 7 were waited for; matrix products, arithmetic and copies ran while one was open for 3% of the time, Pallas kernels for 0%

commit v1 on v0

v1 whole, which is shorter than its diff:
```python
import jax
import jax.numpy as jnp
from jax import lax
from jax.experimental import pallas as pl
from jax.experimental.pallas import tpu as pltpu
from jax.sharding import PartitionSpec as P

HEADS = 8
HEAD_DIM = 128
SPILL = 16
MOST = 32
ROWS = 128
WIDTH = 1024
KEPT = SPILL + MOST
FIRST = ROWS - KEPT
LAST = ROWS - SPILL
QROWS = ROWS + SPILL
KROWS = ROWS + KEPT
NX, NY, NZ = 4, 4, 16
EPSILON = 1e-05
MESH = pl.DeviceIdType.MESH
F32 = jnp.float32
BF16 = jnp.bfloat16


def place():
    dp = lax.axis_index("dp")
    fsdp = lax.axis_index("fsdp")
    return dp // NZ, fsdp // 2, dp % NZ, fsdp % 2


def device(x, y, z, c):
    return (x * NZ + z, y * 2 + c)


def remote(src, dst, send, recv, target):
    return pltpu.make_async_remote_copy(
        src_ref=src, dst_ref=dst, send_sem=send, recv_sem=recv, device_id=target, device_id_type=MESH
    )


def greet(targets):
    barrier = pltpu.get_barrier_semaphore()
    for target in targets:
        pl.semaphore_signal(barrier, inc=1, device_id=target, device_id_type=MESH)
    pl.semaphore_wait(barrier, len(targets))


class Ring:
    def __init__(self, own, view, half, me, towards, other, send, recv):
        ahead, behind, across = (me + 1) % 4, (me + 3) % 4, (me + 2) % 4
        self.first = [
            remote(own, view(me), send.at[0], recv.at[0], towards(ahead)),
            remote(own, view(me), send.at[1], recv.at[1], towards(behind)),
            remote(own, view(me), send.at[4], recv.at[4], other),
        ]
        self.behind = [
            remote(half(behind, 0), half(behind, 0), send.at[2], recv.at[2], towards(ahead)),
            remote(view(behind), view(behind), send.at[5], recv.at[5], other),
        ]
        self.ahead = [
            remote(half(ahead, 1), half(ahead, 1), send.at[3], recv.at[3], towards(behind)),
            remote(view(ahead), view(ahead), send.at[6], recv.at[6], other),
        ]
        self.across = [
            remote(half(across, 0), half(across, 0), send.at[7], recv.at[7], other),
            remote(half(across, 1), half(across, 1), send.at[8], recv.at[8], other),
        ]

    def start(self):
        for copy in self.first:
            copy.start()

    def forward(self):
        self.first[0].wait_recv()
        for copy in self.behind:
            copy.start()
        self.first[1].wait_recv()
        for copy in self.ahead:
            copy.start()

    def finish(self):
        self.behind[0].wait_recv()
        self.across[0].start()
        self.ahead[0].wait_recv()
        self.across[1].start()

    def arrived(self):
        self.first[2].wait_recv()
        self.behind[1].wait_recv()
        self.ahead[1].wait_recv()
        self.across[0].wait_recv()
        self.across[1].wait_recv()

    def sent(self):
        for copy in self.first + self.behind + self.ahead + self.across:
            copy.wait_send()


def gather_kernel(
    mask_ref, actions_ref, cot_ref, w_in_ref, w_out_ref,
    wall_ref, cots_ref, far_ref,
    cot_t, mine, landed,
    wsend, wrecv, csend, crecv, zsend, zrecv, local,
):
    x, y, z, c = place()
    other = device(x, y, z, 1 - c)
    along_y = lambda i: device(x, i, z, c)
    along_x = lambda i: device(i, y, z, c)
    swaps = [device(x, y, z + (1 << k) - 2 * (1 << k) * (z // (1 << k) % 2), c) for k in range(3)]
    greet([along_y((y + 1) % 4), along_y((y + 3) % 4), along_x((x + 1) % 4), along_x((x + 3) % 4), other] + swaps)

    def view(section):
        return lambda i: wall_ref.at[section, pl.ds(pl.multiple_of((2 * i + c) * ROWS, ROWS), ROWS)]

    def half(section):
        return lambda i, h: wall_ref.at[section, pl.ds(pl.multiple_of((2 * i + c) * ROWS + h * 64, 64), 64)]

    rings = []
    own = []
    for t in range(5):
        src = w_in_ref.at[:, t * WIDTH : (t + 1) * WIDTH] if t < 4 else w_out_ref
        rings.append(Ring(src, view(t), half(t), y, along_y, other, wsend.at[t], wrecv.at[t]))
        own.append(pltpu.make_async_copy(src, view(t)(y), local.at[t]))

    cview = lambda i: cots_ref.at[:, pl.ds(pl.multiple_of((2 * i + c) * ROWS, ROWS), ROWS)]
    chalf = lambda i, h: cots_ref.at[h * 512 : h * 512 + 512, pl.ds(pl.multiple_of((2 * i + c) * ROWS, ROWS), ROWS)]
    cring = Ring(cot_t, cview, chalf, x, along_x, other, csend, crecv)
    cown = pltpu.make_async_copy(cot_t, cview(x), local.at[5])
    swap = [
        remote(mine.at[k], landed.at[k], zsend.at[k], zrecv.at[k], swaps[k]) for k in range(3)
    ]

    def turn(k):
        swap[k].wait_recv()
        bit = jnp.full((KEPT + SPILL, WIDTH), lax.shift_right_logical(mask_ref[0, 0], k) & 1, jnp.int32)
        chosen = jnp.where(bit == 1, landed[k].astype(F32), mine[k].astype(F32)).astype(BF16)
        if k < 2:
            mine[k + 1] = chosen
            swap[k + 1].start()
        else:
            far_ref[...] = chosen

    rings[0].start()
    rings[1].start()
    mine[0, :KEPT] = actions_ref[0, FIRST:]
    mine[0, KEPT:] = cot_ref[0, LAST:]
    swap[0].start()
    for copy in own:
        copy.start()
    cot_t[...] = cot_ref[0].astype(F32).T.astype(BF16)
    cring.start()
    cown.start()
    for t in range(5):
        rings[t].forward()
        if t + 2 < 5:
            rings[t + 2].start()
        if t >= 1:
            rings[t - 1].finish()
        if t < 3:
            turn(t)
        if t == 1:
            cring.forward()
        if t == 2:
            cring.finish()
    rings[4].finish()
    for copy in own + [cown]:
        copy.wait()
    for ring in rings + [cring]:
        ring.arrived()
    for ring in rings + [cring]:
        ring.sent()
    for copy in swap:
        copy.wait_send()


def gather(partner_mask, actions, cotangent, w_in, w_out):
    any_space = pl.BlockSpec(memory_space=pl.ANY)
    vmem = pl.BlockSpec(memory_space=pltpu.VMEM)
    return pl.pallas_call(
        gather_kernel,
        out_shape=(
            jax.ShapeDtypeStruct((5, WIDTH, WIDTH), BF16),
            jax.ShapeDtypeStruct((WIDTH, WIDTH), BF16),
            jax.ShapeDtypeStruct((KEPT + SPILL, WIDTH), BF16),
        ),
        in_specs=[pl.BlockSpec(memory_space=pltpu.SMEM), vmem, vmem, any_space, any_space],
        out_specs=(any_space, any_space, vmem),
        scratch_shapes=[
            pltpu.VMEM((WIDTH, ROWS), BF16),
            pltpu.VMEM((3, KEPT + SPILL, WIDTH), BF16),
            pltpu.VMEM((3, KEPT + SPILL, WIDTH), BF16),
            pltpu.SemaphoreType.DMA((5, 9)),
            pltpu.SemaphoreType.DMA((5, 9)),
            pltpu.SemaphoreType.DMA((9,)),
            pltpu.SemaphoreType.DMA((9,)),
            pltpu.SemaphoreType.DMA((3,)),
            pltpu.SemaphoreType.DMA((3,)),
            pltpu.SemaphoreType.DMA((6,)),
        ],
        compiler_params=pltpu.CompilerParams(
            collective_id=0, has_side_effects=True, vmem_limit_bytes=32 * 1024 * 1024
        ),
        name="gather_inputs",
    )(partner_mask, actions, cotangent, w_in, w_out)


def weight_kernel(
    mixed_ref, cots_ref, out_ref,
    all_mixed, total, sums, ybuf, part, zbuf, final, wide,
    msend, mrecv, ysend, yrecv, zsend, zrecv, asend, arecv,
):
    x, y, z, c = place()
    g = 2 * x + c
    group = [((g + d) % 8) for d in range(1, 8)]
    in_group = [device(i // 2, y, z, i % 2) for i in group]
    in_y = [device(x, (y + d) % 4, z, c) for d in range(1, 4)]
    in_z = [device(x, y, (z + d) % 16, c) for d in range(1, 16)]
    ends = [device(y, i // 2, z, i % 2) for i in range(8)]
    begins = [device(i // 2, x, z, i % 2) for i in range(8)]
    barrier = pltpu.get_barrier_semaphore()
    for target in in_group + in_y + in_z:
        pl.semaphore_signal(barrier, inc=1, device_id=target, device_id_type=MESH)
    to_self = [(x == y) & (y == i // 2) & (c == i % 2) for i in range(8)]
    from_self = [(x == y) & (x == i // 2) & (c == i % 2) for i in range(8)]
    for i in range(8):
        @pl.when(jnp.logical_not(to_self[i]))
        def _():
            pl.semaphore_signal(barrier, inc=1, device_id=ends[i], device_id_type=MESH)

        @pl.when(jnp.logical_not(from_self[i]))
        def _():
            pl.semaphore_signal(barrier, inc=1, device_id=begins[i], device_id_type=MESH)
    pl.semaphore_wait(barrier, 7 + 3 + 15 + 16 - 2 * (x == y).astype(jnp.int32))

    spread = []
    for d in range(7):
        copy = remote(
            mixed_ref.at[group[d]], all_mixed.at[pl.ds(pl.multiple_of(g * ROWS, ROWS), ROWS)],
            msend.at[d], mrecv.at[d], in_group[d],
        )
        copy.start()
        spread.append(copy)
    all_mixed[pl.ds(pl.multiple_of(g * ROWS, ROWS), ROWS)] = mixed_ref[g]
    for copy in spread:
        copy.wait()
    total[...] = jnp.dot(cots_ref[...], all_mixed[...], preferred_element_type=F32)
    sums[...] = total[...].astype(BF16)
    copies = []
    for d in range(3):
        to = (y + d + 1) % 4
        copy = remote(sums.at[pl.ds(pl.multiple_of(to * 256, 256), 256)], ybuf.at[d], ysend.at[d], yrecv.at[d], in_y[d])
        copy.start()
        copies.append(copy)
    for copy in copies:
        copy.wait()
    own = total[pl.ds(pl.multiple_of(y * 256, 256), 256)]
    own = own + ybuf[0].astype(F32) + ybuf[1].astype(F32) + ybuf[2].astype(F32)
    part[...] = own.astype(BF16)
    copies = []
    for d in range(15):
        to = (z + d + 1) % 16
        copy = remote(part.at[pl.ds(pl.multiple_of(to * 16, 16), 16)], zbuf.at[d], zsend.at[d], zrecv.at[d], in_z[d])
        copy.start()
        copies.append(copy)
    for copy in copies:
        copy.wait()
    summed = part[pl.ds(pl.multiple_of(z * 16, 16), 16)].astype(F32)
    for d in range(15):
        summed = summed + zbuf[d].astype(F32)
    final[...] = summed * (1.0 / 256.0)
    for i in range(8):
        copy = remote(final, wide.at[g], asend.at[i], arecv.at[g], ends[i])

        @pl.when(jnp.logical_not(to_self[i]))
        def _():
            copy.start()

        @pl.when(to_self[i])
        def _():
            wide[g] = final[...]
    for i in range(8):
        @pl.when(jnp.logical_not(from_self[i]))
        def _():
            remote(final, wide.at[i], asend.at[i], arecv.at[i], begins[i]).wait_recv()

        @pl.when(jnp.logical_not(to_self[i]))
        def _():
            remote(final, wide.at[g], asend.at[i], arecv.at[g], ends[i]).wait_send()
    for i in range(8):
        out_ref[:, i * 128 : (i + 1) * 128] = wide[i]


def weight_sum(mixed_heads, cots):
    vmem = pl.BlockSpec(memory_space=pltpu.VMEM)
    dma = pltpu.SemaphoreType.DMA
    return pl.pallas_call(
        weight_kernel,
        out_shape=jax.ShapeDtypeStruct((16, WIDTH), F32),
        in_specs=[vmem, vmem],
        out_specs=vmem,
        scratch_shapes=[
            pltpu.VMEM((WIDTH, 128), BF16),
            pltpu.VMEM((WIDTH, 128), F32),
            pltpu.VMEM((WIDTH, 128), BF16),
            pltpu.VMEM((3, 256, 128), BF16),
            pltpu.VMEM((256, 128), BF16),
            pltpu.VMEM((15, 16, 128), BF16),
            pltpu.VMEM((16, 128), F32),
            pltpu.VMEM((8, 16, 128), F32),
            dma((7,)), dma((7,)), dma((3,)), dma((3,)), dma((15,)), dma((15,)), dma((8,)), dma((8,)),
        ],
        compiler_params=pltpu.CompilerParams(
            collective_id=1, has_side_effects=True, vmem_limit_bytes=32 * 1024 * 1024
        ),
        name="weight_sum",
    )(mixed_heads, cots)


def normalize(values):
    centred = values - jnp.mean(values, axis=-1, keepdims=True)
    inverse = lax.rsqrt(jnp.mean(centred * centred, axis=-1, keepdims=True) + EPSILON)
    return (centred * inverse, inverse)


def norm_backward(grad, normed, inverse):
    return inverse * (
        grad
        - jnp.mean(grad, axis=-1, keepdims=True)
        - normed * jnp.mean(grad * normed, axis=-1, keepdims=True)
    )


def slope_of(values):
    sigma = jax.nn.sigmoid(values)
    return sigma * (1.0 + values * (1.0 - sigma))


def seen(lengths):
    row = lax.broadcasted_iota(jnp.int32, (QROWS, KROWS), 0)
    column = lax.broadcasted_iota(jnp.int32, (QROWS, KROWS), 1)
    start = jnp.zeros((QROWS, KROWS), jnp.int32)
    end = jnp.zeros((), jnp.int32)
    for k in range(7):
        end = end + lengths[k]
        start = start + jnp.where(row >= end, lengths[k], 0)
    start = jnp.where(row >= FIRST, FIRST, start)
    start = jnp.where(row >= LAST, LAST, start)
    start = jnp.where(row >= ROWS, ROWS, start)
    local = (column >= start) & (column <= row)
    far = (row >= LAST) & (row < ROWS) & (column >= QROWS)
    near = (row >= ROWS) & (column >= FIRST) & (column < LAST)
    return local | far | near


def per_device(actions, lengths, partner_mask, norm_gain, w_in, w_out, cotangent):
    wall, cots, far = gather(partner_mask, actions, cotangent, w_in, w_out)
    inputs = actions[0].astype(F32)
    normed_in, inverse_in = normalize(inputs)
    far_inputs = jnp.concatenate([far[MOST:KEPT], far[:MOST]], axis=0).astype(F32)
    far_normed = normalize(far_inputs)[0]
    normed = (jnp.concatenate([normed_in, far_normed], axis=0) * norm_gain).astype(BF16)
    hidden = jnp.einsum("rk,skn->srn", normed, wall[:4], preferred_element_type=F32)
    active = jax.nn.silu(hidden).astype(BF16)
    gates = active[0, :QROWS].astype(F32)
    heads = lambda a: a.reshape(a.shape[0], HEADS, HEAD_DIM)
    value_heads, query_heads, key_heads = heads(active[1]), heads(active[2, :QROWS]), heads(active[3])
    visible = seen(lengths[0, 0])
    scores = jnp.einsum("qhd,khd->hqk", query_heads, key_heads, preferred_element_type=F32) * HEAD_DIM ** (-0.5)
    weights = (jnp.where(visible[None], jax.nn.silu(scores), 0.0) / MOST).astype(BF16)
    attended = jnp.einsum("hqk,khd->qhd", weights, value_heads, preferred_element_type=F32).reshape(QROWS, WIDTH)
    normed_out, inverse_out = normalize(attended)
    mixed = (normed_out[:ROWS] * gates[:ROWS]).astype(BF16)
    weight_grads = weight_sum(mixed.reshape(ROWS, HEADS, HEAD_DIM).transpose(1, 0, 2), cots)
    output = (jnp.dot(mixed, wall[4], preferred_element_type=F32) + inputs).astype(BF16)
    incoming = jnp.concatenate([cotangent[0], far[KEPT:]], axis=0)
    grad_mixed = lax.dot_general(incoming, wall[4], (((1,), (1,)), ((), ())), preferred_element_type=F32)
    grad_gates = grad_mixed[:ROWS] * normed_out[:ROWS]
    grad_attended = norm_backward(grad_mixed * gates, normed_out, inverse_out).astype(BF16)
    grad_heads = heads(grad_attended)
    grad_w = jnp.einsum("qhd,khd->hqk", grad_heads, value_heads, preferred_element_type=F32)
    grad_scores = (jnp.where(visible[None], grad_w * slope_of(scores), 0.0) * (HEAD_DIM ** (-0.5) / MOST)).astype(BF16)
    grad_queries = jnp.einsum("hqk,khd->qhd", grad_scores[:, :ROWS], key_heads, preferred_element_type=F32)
    grad_keys = jnp.einsum("hqk,qhd->khd", grad_scores[:, :, :ROWS], query_heads, preferred_element_type=F32)
    grad_values = jnp.einsum("hqk,qhd->khd", weights[:, :, :ROWS], grad_heads, preferred_element_type=F32)
    grad_active = jnp.stack(
        [grad_gates] + [g.reshape(ROWS, WIDTH) for g in (grad_values, grad_queries, grad_keys)], axis=0
    )
    grad_hidden = (grad_active * slope_of(hidden[:, :ROWS])).astype(BF16)
    grad_normed = jnp.einsum("srn,skn->rk", grad_hidden, wall[:4], preferred_element_type=F32)
    grad_input = cotangent[0].astype(F32) + norm_backward(grad_normed * norm_gain, normed_in, inverse_in)
    return (output[None], grad_input.astype(BF16)[None], weight_grads)


def solution(mesh):
    placed = (
        P("fsdp", "dp", None),
        P("fsdp", "dp", None),
        P("fsdp", "dp"),
        P(),
        P("fsdp", None),
        P("fsdp", None),
        P("fsdp", "dp", None),
    )
    return jax.shard_map(
        per_device,
        mesh=mesh,
        in_specs=placed,
        out_specs=(P("fsdp", "dp", None), P("fsdp", "dp", None), P("dp", None)),
        check_vma=False,
    )
```

time: 861 us -> 138 us (0.16)
  waiting for transfers between devices: 747 us -> 0 us
  Pallas kernels: 0 us -> 90.2 us
  blocking collectives: 34.5 us -> 0 us
  starting transfers between devices: 30.5 us -> 0 us
  between operations: 14.8 us -> 6.16 us
    unnamed x4 -> x0, waiting for transfers between devices: 649 us -> none
    pallas_call x0 -> x2, Pallas kernels: none -> 90.2 us  [the longest x1 57.2 us: gather(): pl.pallas_call(gather_kernel, out_shape=(jax.ShapeDtypeStruct((5, WIDTH,...]
    all_gather x2 -> x0, waiting for transfers between devices: 60.6 us -> none  [the longest x1 60.6 us: per_device(): in_whole = lax.all_gather(w_in, 'fsdp', axis=0, tiled=True)]
    ppermute x6 -> x0, waiting for transfers between devices: 36.6 us -> none  [swapped(): lax.ppermute(array, axis, [(i, i ^ 1 << distance) for i in range(lax.axis...]
    psum x1 -> x0, blocking collectives: 34.5 us -> none  [per_device(): lax.psum(summed.astype(jnp.bfloat16), 'fsdp').astype(jnp.float32)]
    ppermute x6 -> x0, starting transfers between devices: 30.4 us -> none  [swapped(): lax.ppermute(array, axis, [(i, i ^ 1 << distance) for i in range(lax.axis...]
    dot_general x16 -> x9, matrix products: 18.4 us -> 20.2 us  [the longest x1 8.26 us: per_device(): jnp.einsum('srn,skn->rk', grad_hidden, wall[:4], preferred_element_type=F32)]
  transfers between devices with their start and end apart: 9 -> 0, of which waited for: 7 -> 0; matrix products, arithmetic and copies ran while one was open for 3% -> 0% of each run, Pallas kernels for 0% -> 0%
where the time goes in v1:
time: 138 us; the launch traced here: 137 us
  Pallas kernels  90.2 us (65%)
  matrix products  21.8 us (16%)
  other arithmetic  10.9 us (8%)
  local copies, waits for them, and re-layouts  7.89 us (6%)
  between operations  6.16 us (4%)
    pallas_call x1, Pallas kernels, gather(): pl.pallas_call(gather_kernel, out_shape=(jax.ShapeDtypeStruct((5, WIDTH,...  57.2 us
    pallas_call x1, Pallas kernels, weight_sum(): pl.pallas_call(weight_kernel, out_shape=jax.ShapeDtypeStruct((16, WIDTH),...  33 us
    dot_general x1, matrix products, per_device(): jnp.einsum('srn,skn->rk', grad_hidden, wall[:4], preferred_element_type=F32)  8.26 us
    add x1, other arithmetic, seen(): start = start + jnp.where(row >= end, lengths[k], 0)  4.46 us
    dot_general x1, matrix products, per_device(): jnp.einsum('rk,skn->srn', normed, wall[:4], preferred_element_type=F32)  3.88 us
    unnamed x27, local copies, waits for them, and re-layouts  3.72 us

profile of v1, /device:TPU:1, one launch (start us, length us, event | category | flops | bytes accessed | tf_op | source)
XLA Modules:
  0.0 137.0 jit_solution(14011108426042871095)
XLA Ops:
  1.4 1.1 convert_reduce_fusion
  2.5 1.2 fusion.41
  3.7 1.6 %fusion.90 = (s32[1,1,1]{2,1,0:T(1,128)}, s32[1,1,1]{2,1,0:T(1,128)}, s32[1,1,1]{2,1,0:T(1,128)}, s32[1,1,1]{2,1,0:T(1,128)}, s32[1,1,1]{2,1,0:T(1,128)}, /*index=5*/s32[1,1,1]{2,1,0:T(1,128)}, s32[1,1,1]{2,1,0:T(1,128)}) fusion(s32[1,1,7]{2,1,0:T(1,128)} %param.8), kind=kLoop, calls=%fused_computation.126 | loop fusion | bytes 56 | tf_op jit(solution)/shard_map/slice | solution.py:345
  9.7 4.5 %fusion.82 = s32[144]{0:T(256)S(1)} fusion(s32[]{:T(128)} %bitcast.9, s32[]{:T(128)S(6)} %add.120, s32[]{:T(128)} %bitcast.8, s32[]{:T(128)S(6)} %add.118, s32[]{:T(128)} %bitcast.7, s32[]{:T(128)S(6)} %add.116, s32[]{:T(128)} %bitcast.6, s32[]{:T(128)S(6)} %add.114, s32[]{:T(128)} %bitcast.5, s32[]{:T(128)S(6)} %add.112, s32[]{:T(128)} %bitcast.4, ...), kind=kLoop, calls=%fused_computation.105 | loop fusion | flops 2880 | bytes 628 | tf_op jit(solution)/shard_map/add | solution.py:346
  14.2 0.2 fusion.75
  14.4 1.2 fusion.36
  15.6 0.9 copy-done
  16.5 0.9 copy-done.3
  17.5 0.9 copy-done.5
  18.4 57.2 %gather_inputs.1 = (bf16[5,1024,1024]{2,1,0:T(8,128)(2,1)S(1)}, bf16[1024,1024]{1,0:T(8,128)(2,1)S(1)}, bf16[64,1024]{1,0:T(8,128)(2,1)S(1)}) custom-call(s32[1,1]{1,0:T(1,128)S(6)} %copy.76.mask_ref, bf16[1,128,1024]{2,1,0:T(8,128)(2,1)S(1)} %copy-done, bf16[1,128,1024]{2,1,0:T(8,128)(2,1)S(1)} %copy-done.3, bf16[128,4096]{1,0:T(8,128)(2,1)S(1)} %copy-done.2, ...), custom_call_target="tpu_custom_call" | custom-call | tf_op jit(solution)/shard_map/gather_inputs/pallas_call | solution.py:180
  75.8 0.2 fusion.72
  76.1 3.9 %multiply_convert_fusion = (bf16[4,176,1024]{2,1,0:T(8,128)(2,1)S(1)}, f32[4,176,1024]{2,1,0:T(8,128)}) fusion(bf16[5,1024,1024]{2,1,0:T(8,128)(2,1)S(1)} %get-tuple-element.6, f32[48,1024]{1,0:T(8,128)S(1)} %fusion.70, f32[128,1024]{1,0:T(8,128)S(1)} %fusion.36, f32[1024]{0:T(1024)S(1)} %copy-done.10), kind=kOutput, calls=%fused_computation.4 | convolution fusion | flops 1480540160 | bytes 13438976 | tf_op jit(solution)/shard_map/rk,skn->srn/dot_general | solution.py:363
  80.3 0.7 multiply_convert_fusion.1
  81.0 0.4 fusion.91
  81.4 0.2 fusion.40
  81.7 1.0 fusion.76
  82.7 0.2 fusion.55
  82.9 1.5 %fusion.16 = bf16[8,144,176]{2,1,0:T(8,128)(2,1)} fusion(f32[8,144,176]{2,1,0:T(8,128)S(1)} %get-tuple-element.32, pred[144,176]{1,0:T(8,128)(4,1)S(1)} %fusion.75, bf16[176,8,128]{2,1,0:T(8,128)(2,1)S(1)} %bitcast.123, bf16[18,8,8,128]{3,2,1,0:T(8,128)(2,1)S(1)} %fusion.55), kind=kOutput, calls=%fused_computation.18 | convolution fusion | flops 54134784 | bytes 1897216 | tf_op jit(solution)/shard_map/qhd,khd->hqk/dot_general | solution.py:381
  84.5 1.0 fusion.44
  85.4 0.4 fusion.57
  85.8 1.0 copy.39
  86.8 1.4 %fusion.42 = f32[8,128,128]{2,1,0:T(8,128)S(1)} fusion(bf16[8,144,176]{2,1,0:T(8,128)(2,1)} %fusion.16, bf16[176,8,128]{2,1,0:T(8,128)(2,1)S(1)} %bitcast.121), kind=kOutput, calls=%fused_computation.43 | convolution fusion | flops 46137344 | bytes 1409024 | tf_op jit(solution)/shard_map/hqk,khd->qhd/dot_general | solution.py:383
  88.3 1.4 %fusion.59 = f32[8,128,128]{2,1,0:T(8,128)S(1)} fusion(bf16[8,144,176]{2,1,0:T(8,128)(2,1)} %fusion.16, bf16[144,8,128]{2,1,0:T(8,128)(2,1)} %bitcast.125), kind=kOutput, calls=%fused_computation.65 | convolution fusion | flops 37748736 | bytes 1114112 | tf_op jit(solution)/shard_map/hqk,qhd->khd/dot_general | solution.py:384
  89.7 1.0 copy.41
  90.7 0.2 copy.40
  91.0 8.3 %fusion.87 = (f32[128]{0:T(128)S(1)}, f32[128]{0:T(128)S(1)}, f32[128,1024]{1,0:T(8,128)}) fusion(f32[128]{0:T(128)S(1)} %add_rsqrt_fusion.2, f32[128]{0:T(128)S(1)} %broadcast_multiply_fusion.6, bf16[1,128,1024]{2,1,0:T(8,128)(2,1)S(1)} %copy-done.1, f32[1024]{0:T(1024)S(1)} %copy-done.10, bf16[5,1024,1024]{2,1,0:T(8,128)(2,1)} %copy-done.6, ...), kind=kOutput, calls=%fused_computation.124 | convolution fusion | flops 1080950528 | bytes 13375488 | tf_op jit(solution)/shard_map/srn,skn->rk/dot_general | solution.py:390
  99.2 2.7 %fusion.29 = bf16[1,128,1024]{2,1,0:T(8,128)(2,1)} fusion(bf16[128,1024]{1,0:T(8,128)(2,1)S(1)} %copy-done.8, bf16[5,1024,1024]{2,1,0:T(8,128)(2,1)} %copy-done.6, bf16[1,128,1024]{2,1,0:T(8,128)(2,1)S(1)} %copy-done.1), kind=kOutput, calls=%fused_computation.25 | convolution fusion | flops 268828672 | bytes 2883584 | tf_op jit(solution)/shard_map/dot_general | solution.py:375
  102.0 0.2 copy.36
  102.1 0.2 copy.37
  102.3 33.0 %weight_sum.1 = f32[16,1024]{1,0:T(8,128)S(1)} custom-call(bf16[8,128,128]{2,1,0:T(8,128)(2,1)S(1)} %bitcast.115, bf16[1024,1024]{1,0:T(8,128)(2,1)S(1)} %get-tuple-element.8.cots_ref), custom_call_target="tpu_custom_call" | custom-call | tf_op jit(solution)/shard_map/weight_sum/pallas_call | solution.py:297
  135.4 1.0 fusion.65
  136.3 0.6 copy.77
  (42 shorter events, 0.6 us)
Async XLA Ops:
  0.6 75.5 %copy-start.10 = (f32[1024]{0:T(1024)S(1)}, f32[1024]{0:T(1024)}, u32[]{:S(2)}) copy-start(f32[1024]{0:T(1024)} %param.10) | copy-start | bytes 12292
  0.6 14.9 %copy-start.2 = (bf16[128,4096]{1,0:T(8,128)(2,1)S(1)}, bf16[128,4096]{1,0:T(8,128)(2,1)}, u32[]{:S(2)}) copy-start(bf16[128,4096]{1,0:T(8,128)(2,1)} %w_in_ref.1) | copy-start | bytes 3145732
  15.6 1.0 copy-start
  16.5 0.9 copy-start.3
  17.5 0.9 copy-start.5
  75.7 6.0 %copy-start.6 = (bf16[5,1024,1024]{2,1,0:T(8,128)(2,1)}, bf16[5,1024,1024]{2,1,0:T(8,128)(2,1)S(1)}, u32[]{:S(2)}) copy-start(bf16[5,1024,1024]{2,1,0:T(8,128)(2,1)S(1)} %get-tuple-element.6) | copy-start | bytes 31457284
  80.3 1.3 copy-start.7
  86.8 4.1 %copy-start.1 = (bf16[1,128,1024]{2,1,0:T(8,128)(2,1)S(1)}, bf16[1,128,1024]{2,1,0:T(8,128)(2,1)}, u32[]{:S(2)}) copy-start(bf16[1,128,1024]{2,1,0:T(8,128)(2,1)} %actions_ref.1) | copy-start | bytes 786436
  90.9 8.3 %copy-start.8 = (bf16[128,1024]{1,0:T(8,128)(2,1)S(1)}, bf16[128,1024]{1,0:T(8,128)(2,1)}, u32[]{:S(2)}) copy-start(bf16[128,1024]{1,0:T(8,128)(2,1)} %get-tuple-element.19) | copy-start | bytes 786436
  102.0 33.4 %copy-start.4 = (bf16[1,128,1024]{2,1,0:T(8,128)(2,1)S(1)}, bf16[1,128,1024]{2,1,0:T(8,128)(2,1)}, u32[]{:S(2)}) copy-start(bf16[1,128,1024]{2,1,0:T(8,128)(2,1)} %cot_ref.1) | copy-start | bytes 786436
  102.3 33.0 %copy-start.9 = (f32[128,1024]{1,0:T(8,128)S(1)}, f32[128,1024]{1,0:T(8,128)}, u32[]{:S(2)}) copy-start(f32[128,1024]{1,0:T(8,128)} %get-tuple-element.36) | copy-start | bytes 1572868

commit v2 on v0

v2 whole, which is shorter than its diff:
```python
import jax
import jax.numpy as jnp
from jax import lax
from jax.experimental import pallas as pl
from jax.experimental.pallas import tpu as pltpu
from jax.sharding import PartitionSpec as P

HEADS = 8
HEAD_DIM = 128
SPILL = 16
MOST = 32
ROWS = 128
WIDTH = 1024
LAST = ROWS - SPILL
FIRST = LAST - MOST
NZ = 16
EPSILON = 1e-05
SCALE = HEAD_DIM ** (-0.5)
BACK = SCALE / MOST
MESH = pl.DeviceIdType.MESH
F32 = jnp.float32
BF16 = jnp.bfloat16
GATES, VALUES, QUERIES, KEYS, OUT = range(5)
QUARTER = {QUERIES: 16, KEYS: 16, VALUES: 16, GATES: 32, OUT: 32}
CHUNK = 32
LANES = 256


def device(x, y, z, c):
    return (x * NZ + z, y * 2 + c)


def remote(src, dst, send, recv, target):
    return pltpu.make_async_remote_copy(
        src_ref=src, dst_ref=dst, send_sem=send, recv_sem=recv, device_id=target, device_id_type=MESH
    )


def start_all(copies):
    for copy in copies:
        copy.start()


def dot(a, b):
    return jnp.dot(a, b, preferred_element_type=F32)


def dot_nt(a, b):
    return lax.dot_general(a, b, (((1,), (1,)), ((), ())), preferred_element_type=F32)


def dot_tn(a, b):
    return lax.dot_general(a, b, (((0,), (0,)), ((), ())), preferred_element_type=F32)


def normalize(values):
    centred = values - jnp.mean(values, axis=-1, keepdims=True)
    inverse = lax.rsqrt(jnp.mean(centred * centred, axis=-1, keepdims=True) + EPSILON)
    return (centred * inverse, inverse)


def norm_backward(grad, normed, inverse):
    return inverse * (
        grad
        - jnp.mean(grad, axis=-1, keepdims=True)
        - normed * jnp.mean(grad * normed, axis=-1, keepdims=True)
    )


def silu_parts(values):
    sigma = jax.nn.sigmoid(values)
    return values * sigma, sigma * (1.0 + values * (1.0 - sigma))


class Section:
    def __init__(self, src, wall, t, at, send, recv, local):
        x, y, z, c = at
        quarter = QUARTER[t]
        direct = ROWS - 4 * quarter
        other = device(x, y, z, 1 - c)

        def rows(owner, start, count):
            base = (2 * owner + c) * ROWS + start
            return wall.at[t, pl.ds(pl.multiple_of(base, 16), count)]

        ahead, behind, across = (y + 1) % 4, (y + 3) % 4, (y + 2) % 4
        self.own = pltpu.make_async_copy(src, rows(y, 0, ROWS), local)
        self.first = []
        self.forwards = []
        self.halves = []
        if direct:
            half = direct // 2
            piece = src.at[:direct]
            lane = lambda d, i: device(x, d, z, c)
            self.first += [
                remote(piece, rows(y, 0, direct), send.at[0], recv.at[0], lane(ahead, 0)),
                remote(piece, rows(y, 0, direct), send.at[1], recv.at[1], lane(behind, 0)),
            ]
            self.forwards = [
                remote(rows(behind, 0, half), rows(behind, 0, half), send.at[2], recv.at[2], lane(ahead, 0)),
                remote(rows(ahead, half, half), rows(ahead, half, half), send.at[3], recv.at[3], lane(behind, 0)),
            ]
            self.cores = [
                remote(rows(behind, 0, direct), rows(behind, 0, direct), send.at[5], recv.at[5], other),
                remote(rows(ahead, 0, direct), rows(ahead, 0, direct), send.at[6], recv.at[6], other),
            ]
            self.halves = [
                remote(rows(across, h * half, half), rows(across, h * half, half), send.at[7 + h], recv.at[7 + h], other)
                for h in range(2)
            ]
        self.quarters = []
        self.spread = []
        self.cores_late = []
        place = direct + x * quarter
        for d in range(1, 4):
            to = (y + d) % 4
            source = (y + 4 - d) % 4
            self.quarters.append(
                remote(
                    src.at[pl.ds(pl.multiple_of(place, 16), quarter)], rows(y, place, quarter),
                    send.at[8 + d], recv.at[8 + d], device(x, to, z, c),
                )
            )
            mine = rows(source, place, quarter)
            self.spread.append(
                [
                    remote(
                        mine, mine, send.at[11 + 3 * (d - 1) + e], recv.at[11 + 3 * (d - 1) + e],
                        device((x + e) % 4, y, z, c),
                    )
                    for e in range(1, 4)
                ]
            )
            whole = rows(source, direct, 4 * quarter)
            self.cores_late.append(remote(whole, whole, send.at[20 + d], recv.at[20 + d], other))
        self.to_core = remote(src, rows(y, 0, ROWS), send.at[4], recv.at[4], other)

    def start(self):
        start_all(self.quarters)
        start_all(self.first)
        self.to_core.start()
        self.own.start()

    def forward(self):
        for quarter, spread in zip(self.quarters, self.spread):
            quarter.wait_recv()
            start_all(spread)
        for i, copy in enumerate(self.first):
            copy.wait_recv()
            self.forwards[i].start()
            self.cores[i].start()

    def finish(self):
        for forward, half in zip(self.forwards, self.halves):
            forward.wait_recv()
            half.start()
        for spread, late in zip(self.spread, self.cores_late):
            for copy in spread:
                copy.wait_recv()
            late.start()

    def arrived(self):
        self.own.wait()
        self.to_core.wait_recv()
        if self.first:
            for copy in self.cores + self.halves:
                copy.wait_recv()
        for copy in self.cores_late:
            copy.wait_recv()

    def sent(self):
        copies = self.quarters + sum(self.spread, []) + self.cores_late + [self.to_core]
        if self.first:
            copies += self.first + self.forwards + self.cores + self.halves
        for copy in copies:
            copy.wait_send()


class Ring:
    def __init__(self, own, view, half, me, towards, other, send, recv):
        ahead, behind, across = (me + 1) % 4, (me + 3) % 4, (me + 2) % 4
        self.first = [
            remote(own, view(me), send.at[0], recv.at[0], towards(ahead)),
            remote(own, view(me), send.at[1], recv.at[1], towards(behind)),
            remote(own, view(me), send.at[4], recv.at[4], other),
        ]
        self.behind = [
            remote(half(behind, 0), half(behind, 0), send.at[2], recv.at[2], towards(ahead)),
            remote(view(behind), view(behind), send.at[5], recv.at[5], other),
        ]
        self.ahead = [
            remote(half(ahead, 1), half(ahead, 1), send.at[3], recv.at[3], towards(behind)),
            remote(view(ahead), view(ahead), send.at[6], recv.at[6], other),
        ]
        self.across = [
            remote(half(across, 0), half(across, 0), send.at[7], recv.at[7], other),
            remote(half(across, 1), half(across, 1), send.at[8], recv.at[8], other),
        ]

    def start(self):
        start_all(self.first)

    def forward(self):
        self.first[0].wait_recv()
        start_all(self.behind)
        self.first[1].wait_recv()
        start_all(self.ahead)

    def finish(self):
        self.behind[0].wait_recv()
        self.across[0].start()
        self.ahead[0].wait_recv()
        self.across[1].start()

    def arrived(self):
        for copy in [self.first[2], self.behind[1], self.ahead[1]] + self.across:
            copy.wait_recv()

    def sent(self):
        for copy in self.first + self.behind + self.ahead + self.across:
            copy.wait_send()


class Swap:
    def __init__(self, held, landed, at, order, mask, send, recv):
        x, y, z, c = at
        self.held, self.landed, self.order, self.mask = held, landed, order, mask
        self.copies = []
        for step, bit in enumerate(order):
            size = 1 << bit
            to = z + size - 2 * size * (z // size % 2)
            self.copies.append(
                remote(held.at[step], landed.at[step], send.at[step], recv.at[step], device(x, y, to, c))
            )

    def start(self):
        self.copies[0].start()

    def turn(self, step):
        self.copies[step].wait_recv()
        bit = jnp.full((SPILL, WIDTH), lax.shift_right_logical(self.mask, self.order[step]) & 1, jnp.int32)
        chosen = jnp.where(bit == 1, self.landed[step].astype(F32), self.held[step].astype(F32))
        self.held[step + 1] = chosen.astype(BF16)
        if step < 2:
            self.copies[step + 1].start()

    def sent(self):
        for copy in self.copies:
            copy.wait_send()


def layer_kernel(
    mask_ref, lengths_ref, actions_hbm, gain_hbm, w_in_ref, w_out_ref, cot_hbm,
    output_ref, grad_ref, weight_ref,
    actions, gain, cot, wall, cots, cot_t, normed, normed_in, inverse_in,
    active, slopes, weights, score_slopes, attended, normed_out, inverse_out, mixed,
    far_normed, far_active, grad_att, grad_mix, grad_hidden,
    held, landed, all_mixed, total, sums, xbuf, part, zbuf, final, wide,
    load_sem, wsend, wrecv, wlocal, csend, crecv, clocal, ssend, srecv,
    msend, mrecv, xsend, xrecv, zsend, zrecv, asend, arecv,
):
    dp = lax.axis_index("dp")
    me = lax.axis_index("fsdp")
    x, y, z, c = dp // NZ, me // 2, dp % NZ, me % 2
    at = (x, y, z, c)
    other = device(x, y, z, 1 - c)
    group = [(me + d) % 8 for d in range(1, 8)]
    in_group = [(dp, i) for i in group]
    in_x = [device((x + d) % 4, y, z, c) for d in range(1, 4)]
    in_z = [device(x, y, (z + d) % NZ, c) for d in range(1, NZ)]
    peers = in_group + in_x + in_z

    loads = [
        pltpu.make_async_copy(actions_hbm.at[0], actions, load_sem.at[0]),
        pltpu.make_async_copy(cot_hbm.at[0], cot, load_sem.at[1]),
        pltpu.make_async_copy(gain_hbm, gain, load_sem.at[2]),
    ]
    start_all(loads)
    barrier = pltpu.get_barrier_semaphore()
    for target in peers:
        pl.semaphore_signal(barrier, inc=1, device_id=target, device_id_type=MESH)

    sections = {
        t: Section(
            w_out_ref if t == OUT else w_in_ref.at[:, t * WIDTH : (t + 1) * WIDTH],
            wall, t, at, wsend.at[t], wrecv.at[t], wlocal.at[t],
        )
        for t in range(5)
    }
    column = lambda i: pl.ds(pl.multiple_of((2 * i + c) * ROWS, ROWS), ROWS)
    cring = Ring(
        cot_t,
        lambda i: cots.at[:, column(i)],
        lambda i, h: cots.at[h * 512 : h * 512 + 512, column(i)],
        y, lambda i: device(x, i, z, c), other, csend, crecv,
    )
    cown = pltpu.make_async_copy(cot_t, cots.at[:, column(y)], clocal)
    mask = mask_ref[0, 0]
    orders = [(2, 1, 0), (0, 1, 2), (2, 1, 0), (0, 1, 2)]
    swaps = [Swap(held.at[i], landed.at[i], at, orders[i], mask, ssend.at[i], srecv.at[i]) for i in range(4)]

    for copy in loads:
        copy.wait()
    held[0, 0] = actions[FIRST : FIRST + 16]
    held[1, 0] = actions[FIRST + 16 : LAST]
    held[2, 0] = actions[LAST:]
    held[3, 0] = cot[LAST:]
    pl.semaphore_wait(barrier, len(peers))

    sections[QUERIES].start()
    swaps[0].start()
    swaps[1].start()
    sections[KEYS].start()

    for r in range(0, ROWS, CHUNK):
        n, inverse = normalize(actions[r : r + CHUNK].astype(F32))
        normed_in[r : r + CHUNK] = n
        inverse_in[r : r + CHUNK] = inverse
        normed[r : r + CHUNK] = (n * gain[...]).astype(BF16)
    cot_t[...] = cot[...].astype(F32).T.astype(BF16)
    cown.start()

    row = lax.broadcasted_iota(jnp.int32, (ROWS, ROWS), 0)
    col = lax.broadcasted_iota(jnp.int32, (ROWS, ROWS), 1)
    begin = jnp.zeros((ROWS, ROWS), jnp.int32)
    end = jnp.zeros((), jnp.int32)
    for k in range(7):
        end = end + lengths_ref[0, 0, k]
        begin = begin + jnp.where(row >= end, lengths_ref[0, 0, k], 0)
    begin = jnp.where(row >= FIRST, FIRST, begin)
    begin = jnp.where(row >= LAST, LAST, begin)
    visible = (col >= begin) & (col <= row)

    def project(t):
        for l in range(0, WIDTH, LANES):
            hidden = dot(normed[...], wall[t, :, l : l + LANES])
            value, slope = silu_parts(hidden)
            active[t, :, l : l + LANES] = value.astype(BF16)
            slopes[t, :, l : l + LANES] = slope

    def small(t, rows, first, count):
        for l in range(0, WIDTH, LANES):
            hidden = dot(rows, wall[t, :, l : l + LANES])
            far_active[t, first : first + count, l : l + LANES] = silu_parts(hidden)[0].astype(BF16)

    def head(h):
        return slice(h * HEAD_DIM, (h + 1) * HEAD_DIM)

    swaps[1].turn(0)
    sections[QUERIES].forward()
    sections[VALUES].start()
    swaps[0].turn(0)
    swaps[1].turn(1)
    sections[KEYS].forward()
    sections[GATES].start()
    sections[QUERIES].finish()
    swaps[0].turn(1)
    sections[VALUES].forward()
    sections[KEYS].finish()
    cring.start()
    sections[QUERIES].arrived()
    project(QUERIES)
    swaps[0].turn(2)
    swaps[1].turn(2)
    swaps[2].start()
    swaps[3].start()
    sections[GATES].forward()
    sections[VALUES].finish()
    sections[KEYS].arrived()
    project(KEYS)
    far_inputs = jnp.concatenate([held[0, 3], held[1, 3]], axis=0).astype(F32)
    far_normed[:MOST] = (normalize(far_inputs)[0] * gain[...]).astype(BF16)
    small(KEYS, far_normed[:MOST], 0, MOST)
    sections[GATES].finish()
    sections[OUT].start()
    sections[VALUES].arrived()
    project(VALUES)
    small(VALUES, far_normed[:MOST], 0, MOST)
    cring.forward()
    swaps[3].turn(0)

    far_slopes = []
    for h in range(HEADS):
        q, k, v = active[QUERIES, :, head(h)], active[KEYS, :, head(h)], active[VALUES, :, head(h)]
        value, slope = silu_parts(dot_nt(q, k) * SCALE)
        weight = (jnp.where(visible, value, 0.0) / MOST).astype(BF16)
        weights[h] = weight
        score_slopes[h] = jnp.where(visible, slope, 0.0) * BACK
        value, slope = silu_parts(dot_nt(q[LAST:], far_active[KEYS, :MOST, head(h)]) * SCALE)
        far_slopes.append(slope * BACK)
        far_part = dot((value / MOST).astype(BF16), far_active[VALUES, :MOST, head(h)])
        local_part = dot(weight, v)
        attended[:LAST, head(h)] = local_part[:LAST]
        attended[LAST:, head(h)] = local_part[LAST:] + far_part

    sections[GATES].arrived()
    project(GATES)
    for r in range(0, ROWS, CHUNK):
        n, inverse = normalize(attended[r : r + CHUNK])
        normed_out[r : r + CHUNK] = n
        inverse_out[r : r + CHUNK] = inverse
        mix = (n * active[GATES, r : r + CHUNK].astype(F32)).astype(BF16)
        for h in range(HEADS):
            mixed[h, r : r + CHUNK] = mix[:, head(h)]
    own_rows = pl.ds(pl.multiple_of(me * ROWS, ROWS), ROWS)
    spread = [
        remote(mixed.at[group[d]], all_mixed.at[own_rows], msend.at[d], mrecv.at[d], in_group[d]) for d in range(7)
    ]
    start_all(spread)
    all_mixed[own_rows] = mixed[me]

    cring.finish()
    swaps[2].turn(0)
    swaps[3].turn(1)
    sections[OUT].forward()

    for copy in spread:
        copy.wait_recv()
    cown.wait()
    cring.arrived()
    total[...] = dot(cots[...], all_mixed[...])
    sums[...] = total[...].astype(BF16)
    xcopies = [
        remote(sums.at[pl.ds(pl.multiple_of((x + d + 1) % 4 * 256, 256), 256)], xbuf.at[d], xsend.at[d], xrecv.at[d], in_x[d])
        for d in range(3)
    ]
    start_all(xcopies)

    swaps[2].turn(1)
    sections[OUT].finish()
    sections[OUT].arrived()
    for l in range(0, WIDTH, LANES):
        grad_mix[:, l : l + LANES] = dot_nt(cot[...], wall[OUT, l : l + LANES])

    for copy in xcopies:
        copy.wait_recv()
    part[...] = (
        total[pl.ds(pl.multiple_of(x * 256, 256), 256)]
        + xbuf[0].astype(F32) + xbuf[1].astype(F32) + xbuf[2].astype(F32)
    ).astype(BF16)
    zcopies = [
        remote(part.at[pl.ds(pl.multiple_of((z + d + 1) % NZ * 16, 16), 16)], zbuf.at[d], zsend.at[d], zrecv.at[d], in_z[d])
        for d in range(NZ - 1)
    ]
    start_all(zcopies)

    for r in range(0, ROWS, CHUNK):
        span = slice(r, r + CHUNK)
        grad = grad_mix[span]
        n = normed_out[span]
        grad_hidden[GATES, span] = (grad * n * slopes[GATES, span]).astype(BF16)
        grad_att[span] = norm_backward(
            grad * active[GATES, span].astype(F32), n, inverse_out[span]
        ).astype(BF16)

    swaps[2].turn(2)
    swaps[3].turn(2)
    spill_inputs = held[2, 3].astype(F32)
    far_normed[MOST:] = (normalize(spill_inputs)[0] * gain[...]).astype(BF16)
    for t in (GATES, VALUES, QUERIES, KEYS):
        small(t, far_normed[MOST:], MOST, SPILL)
    near_grad = dot_nt(held[3, 3], wall[OUT])
    rows16 = lax.broadcasted_iota(jnp.int32, (SPILL, SPILL), 0)
    cols16 = lax.broadcasted_iota(jnp.int32, (SPILL, SPILL), 1)
    causal = cols16 <= rows16
    near_weights, near_slopes, near_attended = [], [], []
    for h in range(HEADS):
        q = far_active[QUERIES, MOST:, head(h)]
        value, slope = silu_parts(dot_nt(q, active[KEYS, FIRST:LAST, head(h)]) * SCALE)
        weight = (value / MOST).astype(BF16)
        near_weights.append(weight)
        near_slopes.append(slope * BACK)
        value, _ = silu_parts(dot_nt(q, far_active[KEYS, MOST:, head(h)]) * SCALE)
        weight2 = (jnp.where(causal, value, 0.0) / MOST).astype(BF16)
        near_attended.append(
            dot(weight, active[VALUES, FIRST:LAST, head(h)]) + dot(weight2, far_active[VALUES, MOST:, head(h)])
        )
    near_normed, near_inverse = normalize(jnp.concatenate(near_attended, axis=1))
    near_att = norm_backward(
        near_grad * far_active[GATES, MOST:].astype(F32), near_normed, near_inverse
    ).astype(BF16)

    for h in range(HEADS):
        q, k, v = active[QUERIES, :, head(h)], active[KEYS, :, head(h)], active[VALUES, :, head(h)]
        g = grad_att[:, head(h)]
        grad_s = (dot_nt(g, v) * score_slopes[h]).astype(BF16)
        far_s = (dot_nt(g[LAST:], far_active[VALUES, :MOST, head(h)]) * far_slopes[h]).astype(BF16)
        near_g = near_att[:, head(h)]
        near_s = (dot_nt(near_g, v[FIRST:LAST]) * near_slopes[h]).astype(BF16)
        grad_q = dot(grad_s, k)
        far_q = dot(far_s, far_active[KEYS, :MOST, head(h)])
        grad_k = dot_tn(grad_s, q)
        near_k = dot_tn(near_s, far_active[QUERIES, MOST:, head(h)])
        grad_v = dot_tn(weights[h], g)
        near_v = dot_tn(near_weights[h], near_g)
        slope = slopes[QUERIES, :, head(h)]
        grad_hidden[QUERIES, :LAST, head(h)] = (grad_q[:LAST] * slope[:LAST]).astype(BF16)
        grad_hidden[QUERIES, LAST:, head(h)] = ((grad_q[LAST:] + far_q) * slope[LAST:]).astype(BF16)
        for t, grad, extra in ((KEYS, grad_k, near_k), (VALUES, grad_v, near_v)):
            slope = slopes[t, :, head(h)]
            grad_hidden[t, :FIRST, head(h)] = (grad[:FIRST] * slope[:FIRST]).astype(BF16)
            grad_hidden[t, FIRST:LAST, head(h)] = ((grad[FIRST:LAST] + extra) * slope[FIRST:LAST]).astype(BF16)
            grad_hidden[t, LAST:, head(h)] = (grad[LAST:] * slope[LAST:]).astype(BF16)

    for copy in zcopies:
        copy.wait_recv()
    summed = part[pl.ds(pl.multiple_of(z * 16, 16), 16)].astype(F32)
    for d in range(NZ - 1):
        summed = summed + zbuf[d].astype(F32)
    final[...] = summed * (1.0 / 256.0)
    acopies = [remote(final, wide.at[me], asend.at[d], arecv.at[d], in_group[d]) for d in range(7)]
    start_all(acopies)
    wide[me] = final[...]

    mixed_rows = jnp.concatenate([mixed[h] for h in range(HEADS)], axis=1)
    for l in range(0, WIDTH, LANES):
        output_ref[0, :, l : l + LANES] = (
            dot(mixed_rows, wall[OUT, :, l : l + LANES]) + actions[:, l : l + LANES].astype(F32)
        ).astype(BF16)
    for l in range(0, WIDTH, LANES):
        grad_mix[:, l : l + LANES] = (
            dot_nt(grad_hidden[0], wall[0, l : l + LANES])
            + dot_nt(grad_hidden[1], wall[1, l : l + LANES])
            + dot_nt(grad_hidden[2], wall[2, l : l + LANES])
            + dot_nt(grad_hidden[3], wall[3, l : l + LANES])
        ) * gain[:, l : l + LANES]
    for r in range(0, ROWS, CHUNK):
        span = slice(r, r + CHUNK)
        grad_ref[0, span] = (
            cot[span].astype(F32) + norm_backward(grad_mix[span], normed_in[span], inverse_in[span])
        ).astype(BF16)

    for copy in acopies:
        copy.wait_recv()
    for i in range(8):
        weight_ref[:, i * 128 : (i + 1) * 128] = wide[i]
    for t in range(5):
        sections[t].sent()
    cring.sent()
    for swap in swaps:
        swap.sent()
    for copy in spread + xcopies + zcopies + acopies:
        copy.wait_send()


def per_device(actions, lengths, partner_mask, norm_gain, w_in, w_out, cotangent):
    hbm = pl.BlockSpec(memory_space=pl.ANY)
    vmem = pl.BlockSpec(memory_space=pltpu.VMEM)
    smem = pl.BlockSpec(memory_space=pltpu.SMEM)
    dma = pltpu.SemaphoreType.DMA
    block = (ROWS, WIDTH)
    return pl.pallas_call(
        layer_kernel,
        out_shape=(
            jax.ShapeDtypeStruct((1, ROWS, WIDTH), BF16),
            jax.ShapeDtypeStruct((1, ROWS, WIDTH), BF16),
            jax.ShapeDtypeStruct((16, WIDTH), F32),
        ),
        in_specs=[smem, smem, hbm, hbm, hbm, hbm, hbm],
        out_specs=(vmem, vmem, vmem),
        scratch_shapes=[
            pltpu.VMEM(block, BF16),
            pltpu.VMEM((1, WIDTH), F32),
            pltpu.VMEM(block, BF16),
            pltpu.VMEM((5, WIDTH, WIDTH), BF16),
            pltpu.VMEM((WIDTH, WIDTH), BF16),
            pltpu.VMEM((WIDTH, ROWS), BF16),
            pltpu.VMEM(block, BF16),
            pltpu.VMEM(block, F32),
            pltpu.VMEM((ROWS, 1), F32),
            pltpu.VMEM((4, ROWS, WIDTH), BF16),
            pltpu.VMEM((4, ROWS, WIDTH), F32),
            pltpu.VMEM((HEADS, ROWS, ROWS), BF16),
            pltpu.VMEM((HEADS, ROWS, ROWS), F32),
            pltpu.VMEM(block, F32),
            pltpu.VMEM(block, F32),
            pltpu.VMEM((ROWS, 1), F32),
            pltpu.VMEM((HEADS, ROWS, HEAD_DIM), BF16),
            pltpu.VMEM((MOST + SPILL, WIDTH), BF16),
            pltpu.VMEM((4, MOST + SPILL, WIDTH), BF16),
            pltpu.VMEM(block, BF16),
            pltpu.VMEM(block, F32),
            pltpu.VMEM((4, ROWS, WIDTH), BF16),
            pltpu.VMEM((4, 4, SPILL, WIDTH), BF16),
            pltpu.VMEM((4, 3, SPILL, WIDTH), BF16),
            pltpu.VMEM((WIDTH, 128), BF16),
            pltpu.VMEM((WIDTH, 128), F32),
            pltpu.VMEM((WIDTH, 128), BF16),
            pltpu.VMEM((3, 256, 128), BF16),
            pltpu.VMEM((256, 128), BF16),
            pltpu.VMEM((NZ - 1, 16, 128), BF16),
            pltpu.VMEM((16, 128), F32),
            pltpu.VMEM((8, 16, 128), F32),
            dma((3,)), dma((5, 24)), dma((5, 24)), dma((5,)), dma((9,)), dma((9,)), dma,
            dma((4, 3)), dma((4, 3)), dma((7,)), dma((7,)), dma((3,)), dma((3,)),
            dma((NZ - 1,)), dma((NZ - 1,)), dma((7,)), dma((7,)),
        ],
        compiler_params=pltpu.CompilerParams(
            collective_id=0, has_side_effects=True, vmem_limit_bytes=56 * 1024 * 1024
        ),
        name="layer",
    )(partner_mask, lengths, actions, norm_gain.reshape(1, WIDTH), w_in, w_out, cotangent)


def solution(mesh):
    placed = (
        P("fsdp", "dp", None),
        P("fsdp", "dp", None),
        P("fsdp", "dp"),
        P(),
        P("fsdp", None),
        P("fsdp", None),
        P("fsdp", "dp", None),
    )
    return jax.shard_map(
        per_device,
        mesh=mesh,
        in_specs=placed,
        out_specs=(P("fsdp", "dp", None), P("fsdp", "dp", None), P("dp", None)),
        check_vma=False,
    )
```

time: 861 us -> 84.9 us (0.10)
  waiting for transfers between devices: 747 us -> 0 us
  Pallas kernels: 0 us -> 80.2 us
  blocking collectives: 34.5 us -> 0 us
  starting transfers between devices: 30.5 us -> 0 us
  matrix products: 18.8 us -> 0 us
  between operations: 14.8 us -> 1.3 us
    unnamed x4 -> x0, waiting for transfers between devices: 649 us -> none
    pallas_call x0 -> x1, Pallas kernels: none -> 80.2 us  [per_device(): pl.pallas_call(layer_kernel, out_shape=(jax.ShapeDtypeStruct((1, ROWS, WI...]
    all_gather x2 -> x0, waiting for transfers between devices: 60.6 us -> none  [the longest x1 60.6 us: per_device(): in_whole = lax.all_gather(w_in, 'fsdp', axis=0, tiled=True)]
    ppermute x6 -> x0, waiting for transfers between devices: 36.6 us -> none  [swapped(): lax.ppermute(array, axis, [(i, i ^ 1 << distance) for i in range(lax.axis...]
    psum x1 -> x0, blocking collectives: 34.5 us -> none  [per_device(): lax.psum(summed.astype(jnp.bfloat16), 'fsdp').astype(jnp.float32)]
    ppermute x6 -> x0, starting transfers between devices: 30.4 us -> none  [swapped(): lax.ppermute(array, axis, [(i, i ^ 1 << distance) for i in range(lax.axis...]
    dot_general x17 -> x0, matrix products: 18.8 us -> none  [the longest x1 6.28 us: per_device(): hidden = jnp.dot(normed, in_whole, preferred_element_type=jnp.float32)]
  transfers between devices with their start and end apart: 9 -> 0, of which waited for: 7 -> 0; matrix products, arithmetic and copies ran while one was open for 3% -> 0% of each run, Pallas kernels for 0% -> 0%
where the time goes in v2:
time: 84.9 us; the launch traced here: 84.7 us
  Pallas kernels  80.2 us (94%)
  local copies, waits for them, and re-layouts  3.21 us (4%)
  between operations  1.3 us (2%)
    pallas_call x1, Pallas kernels, per_device(): pl.pallas_call(layer_kernel, out_shape=(jax.ShapeDtypeStruct((1, ROWS, WI...  80.2 us
    unnamed x7, local copies, waits for them, and re-layouts  3.21 us

profile of v2, /device:TPU:1, one launch (start us, length us, event | category | flops | bytes accessed | tf_op | source)
XLA Modules:
  0.0 84.7 jit_solution(11567566998880007310)
XLA Ops:
  1.3 80.2 %layer.1 = (bf16[1,128,1024]{2,1,0:T(8,128)(2,1)}, bf16[1,128,1024]{2,1,0:T(8,128)(2,1)}, f32[16,1024]{1,0:T(8,128)}) custom-call(s32[1,1]{1,0:T(1,128)S(6)} %copy.13.mask_ref, s32[1,1,7]{2,1,0:T(1,128)} %lengths_ref.1, bf16[1,128,1024]{2,1,0:T(8,128)(2,1)} %actions_hbm.1, f32[1,1024]{1,0:T(1,128)} %bitcast.1, bf16[128,4096]{1,0:T(8,128)(2,1)} %w_in_ref.1, ...), custom_call_target="tpu_custom_call" | custom-call | tf_op jit(solution)/shard_map/layer/pallas_call | solution.py:552
  81.4 0.0 copy-start
  81.5 1.7 %copy.14 = bf16[1,128,1024]{2,1,0:T(8,128)(2,1)} copy(bf16[1,128,1024]{2,1,0:T(8,128)(2,1)} %get-tuple-element.6) | data formatting | bytes 524288
  83.2 0.0 copy-done
  83.2 0.0 copy-start.1
  83.2 0.7 copy.15
  83.9 0.2 copy-done.1
  84.0 0.6 copy.16
Async XLA Ops:
  81.4 1.7 %copy-start = (bf16[1,128,1024]{2,1,0:T(8,128)(2,1)S(1)}, bf16[1,128,1024]{2,1,0:T(8,128)(2,1)}, u32[]{:S(2)}) copy-start(bf16[1,128,1024]{2,1,0:T(8,128)(2,1)} %get-tuple-element.7) | copy-start | bytes 786436
  83.2 0.9 %copy-start.1 = (f32[16,1024]{1,0:T(8,128)S(1)}, f32[16,1024]{1,0:T(8,128)}, u32[]{:S(2)}) copy-start(f32[16,1024]{1,0:T(8,128)} %get-tuple-element.8) | copy-start | bytes 196612

commit v3 on v2

--- a/solution.py
+++ b/solution.py
@@ -21,7 +21,14 @@
 F32 = jnp.float32
 BF16 = jnp.bfloat16
 GATES, VALUES, QUERIES, KEYS, OUT = range(5)
-QUARTER = {QUERIES: 16, KEYS: 16, VALUES: 16, GATES: 32, OUT: 32}
+HALF = WIDTH // 2
+PLAN = {
+    QUERIES: (64, [("x", 64, 16, 0, WIDTH)]),
+    KEYS: (0, [("x", 0, 16, 0, WIDTH), ("z", 64, 16, 0, WIDTH)]),
+    VALUES: (0, [("x", 0, 16, 0, WIDTH), ("z", 64, 16, 0, WIDTH)]),
+    GATES: (64, [("x", 64, 16, 0, HALF), ("z", 64, 16, HALF, HALF)]),
+    OUT: (0, [("x", 0, 16, 0, WIDTH), ("z", 64, 16, 0, WIDTH)]),
+}
 CHUNK = 32
 LANES = 256
 
@@ -75,76 +82,89 @@
 class Section:
     def __init__(self, src, wall, t, at, send, recv, local):
         x, y, z, c = at
-        quarter = QUARTER[t]
-        direct = ROWS - 4 * quarter
+        direct, blocks = PLAN[t]
         other = device(x, y, z, 1 - c)
-
-        def rows(owner, start, count):
-            base = (2 * owner + c) * ROWS + start
-            return wall.at[t, pl.ds(pl.multiple_of(base, 16), count)]
+        used = [0]
+
+        def move(piece, target, source=None):
+            slot = used[0]
+            used[0] += 1
+            return remote(piece if source is None else source, piece, send.at[slot], recv.at[slot], target)
+
+        def block(owner, first, count, column=0, columns=WIDTH):
+            base = pl.multiple_of((2 * owner + c) * ROWS + first, 16)
+            return wall.at[t, pl.ds(base, count), column : column + columns]
 
         ahead, behind, across = (y + 1) % 4, (y + 3) % 4, (y + 2) % 4
-        self.own = pltpu.make_async_copy(src, rows(y, 0, ROWS), local)
-        self.first = []
-        self.forwards = []
-        self.halves = []
+        to_ahead, to_behind = device(x, ahead, z, c), device(x, behind, z, c)
+        self.own = pltpu.make_async_copy(src, block(y, 0, ROWS), local)
+        self.to_core = move(block(y, 0, ROWS), other, src)
+        self.first, self.forwards, self.cores, self.halves = [], [], [], []
         if direct:
             half = direct // 2
             piece = src.at[:direct]
-            lane = lambda d, i: device(x, d, z, c)
-            self.first += [
-                remote(piece, rows(y, 0, direct), send.at[0], recv.at[0], lane(ahead, 0)),
-                remote(piece, rows(y, 0, direct), send.at[1], recv.at[1], lane(behind, 0)),
-            ]
-            self.forwards = [
-                remote(rows(behind, 0, half), rows(behind, 0, half), send.at[2], recv.at[2], lane(ahead, 0)),
-                remote(rows(ahead, half, half), rows(ahead, half, half), send.at[3], recv.at[3], lane(behind, 0)),
-            ]
-            self.cores = [
-                remote(rows(behind, 0, direct), rows(behind, 0, direct), send.at[5], recv.at[5], other),
-                remote(rows(ahead, 0, direct), rows(ahead, 0, direct), send.at[6], recv.at[6], other),
-            ]
-            self.halves = [
-                remote(rows(across, h * half, half), rows(across, h * half, half), send.at[7 + h], recv.at[7 + h], other)
-                for h in range(2)
-            ]
-        self.quarters = []
-        self.spread = []
-        self.cores_late = []
-        place = direct + x * quarter
-        for d in range(1, 4):
-            to = (y + d) % 4
-            source = (y + 4 - d) % 4
-            self.quarters.append(
-                remote(
-                    src.at[pl.ds(pl.multiple_of(place, 16), quarter)], rows(y, place, quarter),
-                    send.at[8 + d], recv.at[8 + d], device(x, to, z, c),
+            self.first = [move(block(y, 0, direct), to_ahead, piece), move(block(y, 0, direct), to_behind, piece)]
+            self.forwards = [move(block(behind, 0, half), to_ahead), move(block(ahead, half, half), to_behind)]
+            self.cores = [move(block(behind, 0, direct), other), move(block(ahead, 0, direct), other)]
+            self.halves = [move(block(across, h * half, half), other) for h in range(2)]
+        self.near, self.far, self.spreads = [], [], {}
+        for d, source, to, onward in ((1, behind, to_ahead, to_ahead), (3, ahead, to_behind, to_behind)):
+            for axis, first, count, column, columns in blocks:
+                first = first + (x if axis == "x" else z % 4) * count
+                fetched = move(
+                    block(y, first, count, column, columns), to,
+                    src.at[pl.ds(pl.multiple_of(first, 16), count), column : column + columns],
                 )
-            )
-            mine = rows(source, place, quarter)
-            self.spread.append(
-                [
-                    remote(
-                        mine, mine, send.at[11 + 3 * (d - 1) + e], recv.at[11 + 3 * (d - 1) + e],
-                        device((x + e) % 4, y, z, c),
-                    )
-                    for e in range(1, 4)
-                ]
-            )
-            whole = rows(source, direct, 4 * quarter)
-            self.cores_late.append(remote(whole, whole, send.at[20 + d], recv.at[20 + d], other))
-        self.to_core = remote(src, rows(y, 0, ROWS), send.at[4], recv.at[4], other)
+                part = columns // 2
+                passed = move(block(source, first, count, column + (part if d == 3 else 0), part), onward)
+                self.near.append((fetched, passed))
+        for d, source in ((1, behind), (3, ahead), (2, across)):
+            self.spreads[d] = []
+            for axis, first, count, column, columns in blocks:
+                first = first + (x if axis == "x" else z % 4) * count
+                whole = block(source, first, count, column, columns)
+                if axis == "x":
+                    spread = [move(whole, device((x + e) % 4, y, z, c)) for e in (2, 1, 3)]
+                else:
+                    part = columns // 2
+                    spread = [
+                        move(block(source, first, count, column, part), device(x, y, (z + 2) % NZ, c)),
+                        move(block(source, first, count, column + part, part), device(x, y, (z + NZ - 2) % NZ, c)),
+                        move(whole, device(x, y, (z + 1) % NZ, c)),
+                        move(whole, device(x, y, (z + NZ - 1) % NZ, c)),
+                    ]
+                self.spreads[d].append(spread)
+        self.late = {d: move(block((y + 4 - d) % 4, direct, ROWS - direct), other) for d in (1, 3, 2)}
+
+    def fetch(self):
+        for fetched, _ in self.near:
+            fetched.start()
 
     def start(self):
-        start_all(self.quarters)
         start_all(self.first)
         self.to_core.start()
         self.own.start()
 
+    def spread(self):
+        for (fetched, passed), spread in zip(self.near, self.spreads[1] + self.spreads[3]):
+            fetched.wait_recv()
+            passed.start()
+            start_all(spread)
+
+    def across(self):
+        kinds = len(self.spreads[2])
+        for i, spread in enumerate(self.spreads[2]):
+            self.near[i][1].wait_recv()
+            self.near[kinds + i][1].wait_recv()
+            start_all(spread)
+
+    def collect(self):
+        for d, late in self.late.items():
+            for copy in sum(self.spreads[d], []):
+                copy.wait_recv()
+            late.start()
+
     def forward(self):
-        for quarter, spread in zip(self.quarters, self.spread):
-            quarter.wait_recv()
-            start_all(spread)
         for i, copy in enumerate(self.first):
             copy.wait_recv()
             self.forwards[i].start()
@@ -154,24 +174,17 @@
         for forward, half in zip(self.forwards, self.halves):
             forward.wait_recv()
             half.start()
-        for spread, late in zip(self.spread, self.cores_late):
-            for copy in spread:
-                copy.wait_recv()
-            late.start()
 
     def arrived(self):
         self.own.wait()
-        self.to_core.wait_recv()
-        if self.first:
-            for copy in self.cores + self.halves:
-                copy.wait_recv()
-        for copy in self.cores_late:
+        for copy in [self.to_core] + self.cores + self.halves + list(self.late.values()):
             copy.wait_recv()
 
     def sent(self):
-        copies = self.quarters + sum(self.spread, []) + self.cores_late + [self.to_core]
-        if self.first:
-            copies += self.first + self.forwards + self.cores + self.halves
+        copies = [self.to_core] + self.first + self.forwards + self.cores + self.halves
+        copies += list(self.late.values()) + sum(sum(self.spreads.values(), []), [])
+        for fetched, passed in self.near:
+            copies += [fetched, passed]
         for copy in copies:
             copy.wait_send()
 
@@ -238,7 +251,7 @@
 
     def turn(self, step):
         self.copies[step].wait_recv()
-        bit = jnp.full((SPILL, WIDTH), lax.shift_right_logical(self.mask, self.order[step]) & 1, jnp.int32)
+        bit = jnp.full((SPILL, WIDTH), lax.shift_right_logical(self.mask[0, 0], self.order[step]) & 1, jnp.int32)
         chosen = jnp.where(bit == 1, self.landed[step].astype(F32), self.held[step].astype(F32))
         self.held[step + 1] = chosen.astype(BF16)
         if step < 2:
@@ -250,8 +263,9 @@
 
 
 def layer_kernel(
-    mask_ref, lengths_ref, actions_hbm, gain_hbm, w_in_ref, w_out_ref, cot_hbm,
-    output_ref, grad_ref, weight_ref,
+    mask_hbm, lengths_hbm, actions_hbm, gain_hbm, w_in_ref, w_out_ref, cot_hbm,
+    output_hbm, grad_hbm, weight_hbm,
+    mask_ref, lengths_ref, output, grad_input, weight_grad, store_sem,
     actions, gain, cot, wall, cots, cot_t, normed, normed_in, inverse_in,
     active, slopes, weights, score_slopes, attended, normed_out, inverse_out, mixed,
     far_normed, far_active, grad_att, grad_mix, grad_hidden,
@@ -274,6 +288,8 @@
         pltpu.make_async_copy(actions_hbm.at[0], actions, load_sem.at[0]),
         pltpu.make_async_copy(cot_hbm.at[0], cot, load_sem.at[1]),
         pltpu.make_async_copy(gain_hbm, gain, load_sem.at[2]),
+        pltpu.make_async_copy(mask_hbm, mask_ref, load_sem.at[3]),
+        pltpu.make_async_copy(lengths_hbm, lengths_ref, load_sem.at[4]),
     ]
     start_all(loads)
     barrier = pltpu.get_barrier_semaphore()
@@ -295,22 +311,22 @@
         y, lambda i: device(x, i, z, c), other, csend, crecv,
     )
     cown = pltpu.make_async_copy(cot_t, cots.at[:, column(y)], clocal)
-    mask = mask_ref[0, 0]
     orders = [(2, 1, 0), (0, 1, 2), (2, 1, 0), (0, 1, 2)]
-    swaps = [Swap(held.at[i], landed.at[i], at, orders[i], mask, ssend.at[i], srecv.at[i]) for i in range(4)]
-
+    swaps = [Swap(held.at[i], landed.at[i], at, orders[i], mask_ref, ssend.at[i], srecv.at[i]) for i in range(4)]
+
+    pl.semaphore_wait(barrier, len(peers))
+    sections[QUERIES].fetch()
     for copy in loads:
         copy.wait()
     held[0, 0] = actions[FIRST : FIRST + 16]
     held[1, 0] = actions[FIRST + 16 : LAST]
     held[2, 0] = actions[LAST:]
     held[3, 0] = cot[LAST:]
-    pl.semaphore_wait(barrier, len(peers))
-
-    sections[QUERIES].start()
     swaps[0].start()
     swaps[1].start()
-    sections[KEYS].start()
+    sections[KEYS].fetch()
+    sections[VALUES].fetch()
+    sections[GATES].fetch()
 
     for r in range(0, ROWS, CHUNK):
         n, inverse = normalize(actions[r : r + CHUNK].astype(F32))
@@ -346,38 +362,47 @@
     def head(h):
         return slice(h * HEAD_DIM, (h + 1) * HEAD_DIM)
 
+    sections[QUERIES].spread()
+    sections[KEYS].spread()
+    sections[KEYS].start()
+    sections[VALUES].start()
     swaps[1].turn(0)
+    sections[VALUES].spread()
+    sections[QUERIES].start()
+    sections[QUERIES].across()
+    swaps[0].turn(0)
+    sections[KEYS].across()
+    sections[GATES].spread()
+    sections[GATES].start()
+    sections[VALUES].across()
+    sections[GATES].across()
+    swaps[1].turn(1)
     sections[QUERIES].forward()
-    sections[VALUES].start()
-    swaps[0].turn(0)
-    swaps[1].turn(1)
-    sections[KEYS].forward()
-    sections[GATES].start()
+    swaps[0].turn(1)
+    sections[GATES].forward()
+    cring.start()
+    sections[OUT].fetch()
+    sections[QUERIES].collect()
+    sections[KEYS].collect()
     sections[QUERIES].finish()
-    swaps[0].turn(1)
-    sections[VALUES].forward()
-    sections[KEYS].finish()
-    cring.start()
+    sections[VALUES].collect()
+    sections[KEYS].arrived()
+    project(KEYS)
     sections[QUERIES].arrived()
     project(QUERIES)
     swaps[0].turn(2)
     swaps[1].turn(2)
     swaps[2].start()
     swaps[3].start()
-    sections[GATES].forward()
-    sections[VALUES].finish()
-    sections[KEYS].arrived()
-    project(KEYS)
     far_inputs = jnp.concatenate([held[0, 3], held[1, 3]], axis=0).astype(F32)
     far_normed[:MOST] = (normalize(far_inputs)[0] * gain[...]).astype(BF16)
     small(KEYS, far_normed[:MOST], 0, MOST)
     sections[GATES].finish()
-    sections[OUT].start()
     sections[VALUES].arrived()
     project(VALUES)
     small(VALUES, far_normed[:MOST], 0, MOST)
+    sections[GATES].collect()
     cring.forward()
-    swaps[3].turn(0)
 
     far_slopes = []
     for h in range(HEADS):
@@ -408,58 +433,37 @@
     ]
     start_all(spread)
     all_mixed[own_rows] = mixed[me]
-
+    swaps[3].turn(0)
+    swaps[2].turn(0)
+    sections[OUT].spread()
+    sections[OUT].start()
     cring.finish()
-    swaps[2].turn(0)
     swaps[3].turn(1)
-    sections[OUT].forward()
+    swaps[2].turn(1)
 
     for copy in spread:
         copy.wait_recv()
     cown.wait()
     cring.arrived()
-    total[...] = dot(cots[...], all_mixed[...])
-    sums[...] = total[...].astype(BF16)
-    xcopies = [
-        remote(sums.at[pl.ds(pl.multiple_of((x + d + 1) % 4 * 256, 256), 256)], xbuf.at[d], xsend.at[d], xrecv.at[d], in_x[d])
-        for d in range(3)
-    ]
-    start_all(xcopies)
-
-    swaps[2].turn(1)
-    sections[OUT].finish()
-    sections[OUT].arrived()
-    for l in range(0, WIDTH, LANES):
-        grad_mix[:, l : l + LANES] = dot_nt(cot[...], wall[OUT, l : l + LANES])
-
-    for copy in xcopies:
-        copy.wait_recv()
-    part[...] = (
-        total[pl.ds(pl.multiple_of(x * 256, 256), 256)]
-        + xbuf[0].astype(F32) + xbuf[1].astype(F32) + xbuf[2].astype(F32)
-    ).astype(BF16)
-    zcopies = [
-        remote(part.at[pl.ds(pl.multiple_of((z + d + 1) % NZ * 16, 16), 16)], zbuf.at[d], zsend.at[d], zrecv.at[d], in_z[d])
-        for d in range(NZ - 1)
-    ]
-    start_all(zcopies)
-
-    for r in range(0, ROWS, CHUNK):
-        span = slice(r, r + CHUNK)
-        grad = grad_mix[span]
-        n = normed_out[span]
-        grad_hidden[GATES, span] = (grad * n * slopes[GATES, span]).astype(BF16)
-        grad_att[span] = norm_backward(
-            grad * active[GATES, span].astype(F32), n, inverse_out[span]
-        ).astype(BF16)
-
+    xcopies = []
+    for d in (2, 1, 3, 0):
+        quarter = pl.ds(pl.multiple_of((x + d) % 4 * 256, 256), 256)
+        product = dot(cots[quarter], all_mixed[...])
+        if d:
+            sums[quarter] = product.astype(BF16)
+            copy = remote(sums.at[quarter], xbuf.at[d - 1], xsend.at[d - 1], xrecv.at[d - 1], in_x[d - 1])
+            copy.start()
+            xcopies.append(copy)
+        else:
+            total[...] = product
+
+    sections[OUT].across()
     swaps[2].turn(2)
     swaps[3].turn(2)
     spill_inputs = held[2, 3].astype(F32)
     far_normed[MOST:] = (normalize(spill_inputs)[0] * gain[...]).astype(BF16)
     for t in (GATES, VALUES, QUERIES, KEYS):
         small(t, far_normed[MOST:], MOST, SPILL)
-    near_grad = dot_nt(held[3, 3], wall[OUT])
     rows16 = lax.broadcasted_iota(jnp.int32, (SPILL, SPILL), 0)
     cols16 = lax.broadcasted_iota(jnp.int32, (SPILL, SPILL), 1)
     causal = cols16 <= rows16
@@ -475,6 +479,44 @@
         near_attended.append(
             dot(weight, active[VALUES, FIRST:LAST, head(h)]) + dot(weight2, far_active[VALUES, MOST:, head(h)])
         )
+    for copy in xcopies:
+        copy.wait_recv()
+    part[...] = (
+        total[...] + xbuf[0].astype(F32) + xbuf[1].astype(F32) + xbuf[2].astype(F32)
+    ).astype(BF16)
+    zcopies = [
+        remote(part.at[pl.ds(pl.multiple_of((z + d + 1) % NZ * 16, 16), 16)], zbuf.at[d], zsend.at[d], zrecv.at[d], in_z[d])
+        for d in range(NZ - 1)
+    ]
+    for d in (7, 6, 8, 5, 9, 4, 10, 3, 11, 2, 12, 1, 13, 0, 14):
+        zcopies[d].start()
+
+    sections[OUT].collect()
+    sections[OUT].arrived()
+    for l in range(0, WIDTH, LANES):
+        grad_mix[:, l : l + LANES] = dot_nt(cot[...], wall[OUT, l : l + LANES])
+
+    for r in range(0, ROWS, CHUNK):
+        span = slice(r, r + CHUNK)
+        grad = grad_mix[span]
+        n = normed_out[span]
+        grad_hidden[GATES, span] = (grad * n * slopes[GATES, span]).astype(BF16)
+        grad_att[span] = norm_backward(
+            grad * active[GATES, span].astype(F32), n, inverse_out[span]
+        ).astype(BF16)
+
+    mixed_rows = jnp.concatenate([mixed[h] for h in range(HEADS)], axis=1)
+    for l in range(0, WIDTH, LANES):
+        output[:, l : l + LANES] = (
+            dot(mixed_rows, wall[OUT, :, l : l + LANES]) + actions[:, l : l + LANES].astype(F32)
+        ).astype(BF16)
+    stores = [
+        pltpu.make_async_copy(output, output_hbm.at[0], store_sem.at[0]),
+        pltpu.make_async_copy(grad_input, grad_hbm.at[0], store_sem.at[1]),
+        pltpu.make_async_copy(weight_grad, weight_hbm, store_sem.at[2]),
+    ]
+    stores[0].start()
+    near_grad = dot_nt(held[3, 3], wall[OUT])
     near_normed, near_inverse = normalize(jnp.concatenate(near_attended, axis=1))
     near_att = norm_backward(
         near_grad * far_active[GATES, MOST:].astype(F32), near_normed, near_inverse
@@ -512,11 +554,6 @@
     start_all(acopies)
     wide[me] = final[...]
 
-    mixed_rows = jnp.concatenate([mixed[h] for h in range(HEADS)], axis=1)
-    for l in range(0, WIDTH, LANES):
-        output_ref[0, :, l : l + LANES] = (
-            dot(mixed_rows, wall[OUT, :, l : l + LANES]) + actions[:, l : l + LANES].astype(F32)
-        ).astype(BF16)
     for l in range(0, WIDTH, LANES):
         grad_mix[:, l : l + LANES] = (
             dot_nt(grad_hidden[0], wall[0, l : l + LANES])
@@ -526,39 +563,62 @@
         ) * gain[:, l : l + LANES]
     for r in range(0, ROWS, CHUNK):
         span = slice(r, r + CHUNK)
-        grad_ref[0, span] = (
+        grad_input[span] = (
             cot[span].astype(F32) + norm_backward(grad_mix[span], normed_in[span], inverse_in[span])
         ).astype(BF16)
 
+    stores[1].start()
+    for section in sections.values():
+        section.sent()
+    cring.sent()
+    for swap in swaps:
+        swap.sent()
+    for copy in spread + xcopies + zcopies:
+        copy.wait_send()
     for copy in acopies:
         copy.wait_recv()
     for i in range(8):
-        weight_ref[:, i * 128 : (i + 1) * 128] = wide[i]
-    for t in range(5):
-        sections[t].sent()
-    cring.sent()
-    for swap in swaps:
-        swap.sent()
-    for copy in spread + xcopies + zcopies + acopies:
+        weight_grad[:, i * 128 : (i + 1) * 128] = wide[i]
+    stores[2].start()
+    for copy in acopies:
         copy.wait_send()
+    for copy in stores:
+        copy.wait()
+
+
+def publish_kernel(*refs):
+    sources, results, staged, load_sem, store_sem = refs[:3], refs[3:6], refs[6:9], refs[9], refs[10]
+    loads = [pltpu.make_async_copy(sources[i], staged[i], load_sem.at[i]) for i in range(3)]
+    stores = [pltpu.make_async_copy(staged[i], results[i], store_sem.at[i]) for i in range(3)]
+    start_all(loads)
+    for load, store in zip(loads, stores):
+        load.wait()
+        store.start()
+    for store in stores:
+        store.wait()
 
 
 def per_device(actions, lengths, partner_mask, norm_gain, w_in, w_out, cotangent):
     hbm = pl.BlockSpec(memory_space=pl.ANY)
-    vmem = pl.BlockSpec(memory_space=pltpu.VMEM)
-    smem = pl.BlockSpec(memory_space=pltpu.SMEM)
     dma = pltpu.SemaphoreType.DMA
     block = (ROWS, WIDTH)
-    return pl.pallas_call(
+    shapes = (
+        jax.ShapeDtypeStruct((1, ROWS, WIDTH), BF16),
+        jax.ShapeDtypeStruct((1, ROWS, WIDTH), BF16),
+        jax.ShapeDtypeStruct((16, WIDTH), F32),
+    )
+    results = pl.pallas_call(
         layer_kernel,
-        out_shape=(
-            jax.ShapeDtypeStruct((1, ROWS, WIDTH), BF16),
-            jax.ShapeDtypeStruct((1, ROWS, WIDTH), BF16),
-            jax.ShapeDtypeStruct((16, WIDTH), F32),
-        ),
-        in_specs=[smem, smem, hbm, hbm, hbm, hbm, hbm],
-        out_specs=(vmem, vmem, vmem),
+        out_shape=shapes,
+        in_specs=[hbm] * 7,
+        out_specs=(hbm, hbm, hbm),
         scratch_shapes=[
+            pltpu.SMEM((1, 1), jnp.int32),
+            pltpu.SMEM((1, 1, 7), jnp.int32),
+            pltpu.VMEM(block, BF16),
+            pltpu.VMEM(block, BF16),
+            pltpu.VMEM((16, WIDTH), F32),
+            dma((3,)),
             pltpu.VMEM(block, BF16),
             pltpu.VMEM((1, WIDTH), F32),
             pltpu.VMEM(block, BF16),
@@ -584,14 +644,14 @@
             pltpu.VMEM((4, 4, SPILL, WIDTH), BF16),
             pltpu.VMEM((4, 3, SPILL, WIDTH), BF16),
             pltpu.VMEM((WIDTH, 128), BF16),
-            pltpu.VMEM((WIDTH, 128), F32),
+            pltpu.VMEM((256, 128), F32),
             pltpu.VMEM((WIDTH, 128), BF16),
             pltpu.VMEM((3, 256, 128), BF16),
             pltpu.VMEM((256, 128), BF16),
             pltpu.VMEM((NZ - 1, 16, 128), BF16),
             pltpu.VMEM((16, 128), F32),
             pltpu.VMEM((8, 16, 128), F32),
-            dma((3,)), dma((5, 24)), dma((5, 24)), dma((5,)), dma((9,)), dma((9,)), dma,
+            dma((5,)), dma((5, 42)), dma((5, 42)), dma((5,)), dma((9,)), dma((9,)), dma,
             dma((4, 3)), dma((4, 3)), dma((7,)), dma((7,)), dma((3,)), dma((3,)),
             dma((NZ - 1,)), dma((NZ - 1,)), dma((7,)), dma((7,)),
         ],
@@ -600,6 +660,15 @@
         ),
         name="layer",
     )(partner_mask, lengths, actions, norm_gain.reshape(1, WIDTH), w_in, w_out, cotangent)
+    return pl.pallas_call(
+        publish_kernel,
+        out_shape=shapes,
+        in_specs=[hbm, hbm, hbm],
+        out_specs=(hbm, hbm, hbm),
+        scratch_shapes=[pltpu.VMEM(shape.shape, shape.dtype) for shape in shapes] + [dma((3,)), dma((3,))],
+        compiler_params=pltpu.CompilerParams(vmem_limit_bytes=60 * 1024 * 1024),
+        name="publish",
+    )(*results)
 
 
 def solution(mesh):

time: 84.9 us -> 74.9 us (0.88)
  Pallas kernels: 80.2 us -> 73.5 us
  local copies, waits for them, and re-layouts: 3.21 us -> 0 us
    pallas_call x1 -> x2, Pallas kernels: 80.2 us -> 73.5 us  [the longest x1 71.7 us: per_device(): pl.pallas_call(layer_kernel, out_shape=shapes, in_specs=[hbm] * 7, out_sp...]
    unnamed x7 -> x0, local copies, waits for them, and re-layouts: 3.21 us -> none
where the time goes in v3:
time: 74.9 us; the launch traced here: 74.8 us
  Pallas kernels  73.5 us (98%)
  between operations  1.29 us (2%)
    pallas_call x1, Pallas kernels, per_device(): pl.pallas_call(layer_kernel, out_shape=shapes, in_specs=[hbm] * 7, out_sp...  71.7 us
    pallas_call x1, Pallas kernels, per_device(): pl.pallas_call(publish_kernel, out_shape=shapes, in_specs=[hbm, hbm, hbm]...  1.8 us

profile of v3, /device:TPU:1, one launch (start us, length us, event | category | flops | bytes accessed | tf_op | source)
XLA Modules:
  0.0 74.8 jit_solution(17035429826923242150)
XLA Ops:
  1.3 71.7 %layer.1 = (bf16[1,128,1024]{2,1,0:T(8,128)(2,1)}, bf16[1,128,1024]{2,1,0:T(8,128)(2,1)}, f32[16,1024]{1,0:T(8,128)}) custom-call(s32[1,1]{1,0:T(1,128)S(6)} %copy.10.mask_hbm, s32[1,1,7]{2,1,0:T(1,128)} %lengths_hbm.1, bf16[1,128,1024]{2,1,0:T(8,128)(2,1)} %actions_hbm.1, f32[1,1024]{1,0:T(1,128)} %bitcast.1, bf16[128,4096]{1,0:T(8,128)(2,1)} %w_in_ref.1, ...), custom_call_target="tpu_custom_call" | custom-call | tf_op jit(solution)/shard_map/layer/pallas_call | solution.py:610
  73.0 1.8 %publish.1 = (bf16[1,128,1024]{2,1,0:T(8,128)(2,1)}, bf16[1,128,1024]{2,1,0:T(8,128)(2,1)}, f32[16,1024]{1,0:T(8,128)}) custom-call(bf16[1,128,1024]{2,1,0:T(8,128)(2,1)} %get-tuple-element.6.refs_0_, bf16[1,128,1024]{2,1,0:T(8,128)(2,1)} %get-tuple-element.7.refs_1_, f32[16,1024]{1,0:T(8,128)} %get-tuple-element.8.refs_2_), custom_call_target="tpu_custom_call" | custom-call | tf_op jit(solution)/shard_map/publish/pallas_call | solution.py:663

commit v4 on v3

--- a/solution.py
+++ b/solution.py
@@ -29,6 +29,7 @@
     GATES: (64, [("x", 64, 16, 0, HALF), ("z", 64, 16, HALF, HALF)]),
     OUT: (0, [("x", 0, 16, 0, WIDTH), ("z", 64, 16, 0, WIDTH)]),
 }
+SEMAPHORES = 86
 CHUNK = 32
 LANES = 256
 
@@ -79,17 +80,26 @@
     return values * sigma, sigma * (1.0 + values * (1.0 - sigma))
 
 
+def await_received(ref, sem, target):
+    remote(ref, ref, sem, sem, target).wait_recv()
+
+
+def await_sent(ref, sem, target):
+    remote(ref, ref, sem, sem, target).wait_send()
+
+
 class Section:
-    def __init__(self, src, wall, t, at, send, recv, local):
+    def __init__(self, src, wall, t, at, new):
         x, y, z, c = at
         direct, blocks = PLAN[t]
         other = device(x, y, z, 1 - c)
-        used = [0]
-
-        def move(piece, target, source=None):
-            slot = used[0]
-            used[0] += 1
-            return remote(piece if source is None else source, piece, send.at[slot], recv.at[slot], target)
+        sent = new()
+        self.send, self.other, self.wall = sent, other, wall.at[t]
+        self.rows_sent = 0
+
+        def move(piece, target, recv, source=None):
+            self.rows_sent += piece.shape[0] * piece.shape[1] // WIDTH
+            return remote(piece if source is None else source, piece, sent, recv, target)
 
         def block(owner, first, count, column=0, columns=WIDTH):
             base = pl.multiple_of((2 * owner + c) * ROWS + first, 16)
@@ -97,48 +107,62 @@
 
         ahead, behind, across = (y + 1) % 4, (y + 3) % 4, (y + 2) % 4
         to_ahead, to_behind = device(x, ahead, z, c), device(x, behind, z, c)
-        self.own = pltpu.make_async_copy(src, block(y, 0, ROWS), local)
-        self.to_core = move(block(y, 0, ROWS), other, src)
+        self.own = pltpu.make_async_copy(src, block(y, 0, ROWS), new())
+        self.core = new()
+        self.to_core = move(block(y, 0, ROWS), other, self.core, src)
         self.first, self.forwards, self.cores, self.halves = [], [], [], []
         if direct:
             half = direct // 2
             piece = src.at[:direct]
-            self.first = [move(block(y, 0, direct), to_ahead, piece), move(block(y, 0, direct), to_behind, piece)]
-            self.forwards = [move(block(behind, 0, half), to_ahead), move(block(ahead, half, half), to_behind)]
-            self.cores = [move(block(behind, 0, direct), other), move(block(ahead, 0, direct), other)]
-            self.halves = [move(block(across, h * half, half), other) for h in range(2)]
-        self.near, self.far, self.spreads = [], [], {}
-        for d, source, to, onward in ((1, behind, to_ahead, to_ahead), (3, ahead, to_behind, to_behind)):
+            self.first = [
+                move(block(y, 0, direct), to_ahead, new(), piece), move(block(y, 0, direct), to_behind, new(), piece)
+            ]
+            self.forwards = [
+                move(block(behind, 0, half), to_ahead, new()), move(block(ahead, half, half), to_behind, new())
+            ]
+            self.cores = [
+                move(block(behind, 0, direct), other, self.core), move(block(ahead, 0, direct), other, self.core)
+            ]
+            self.halves = [move(block(across, h * half, half), other, self.core) for h in range(2)]
+        self.fetched, self.passed, self.spreads, self.late = {}, {}, {}, {}
+        self.near, self.far, self.spread_sem = {1: new(), 3: new()}, new(), {d: new() for d in (1, 3, 2)}
+        self.block_rows = sum(count * columns // WIDTH for _, _, count, _, columns in blocks)
+        for d, source, to in ((1, behind, to_ahead), (3, ahead, to_behind)):
+            self.fetched[d], self.passed[d] = [], []
             for axis, first, count, column, columns in blocks:
                 first = first + (x if axis == "x" else z % 4) * count
-                fetched = move(
-                    block(y, first, count, column, columns), to,
-                    src.at[pl.ds(pl.multiple_of(first, 16), count), column : column + columns],
+                self.fetched[d].append(
+                    move(
+                        block(y, first, count, column, columns), to, self.near[d],
+                        src.at[pl.ds(pl.multiple_of(first, 16), count), column : column + columns],
+                    )
                 )
                 part = columns // 2
-                passed = move(block(source, first, count, column + (part if d == 3 else 0), part), onward)
-                self.near.append((fetched, passed))
+                start = column + (part if d == 3 else 0)
+                self.passed[d].append(move(block(source, first, count, start, part), to, self.far))
         for d, source in ((1, behind), (3, ahead), (2, across)):
             self.spreads[d] = []
+            sem = self.spread_sem[d]
             for axis, first, count, column, columns in blocks:
                 first = first + (x if axis == "x" else z % 4) * count
                 whole = block(source, first, count, column, columns)
                 if axis == "x":
-                    spread = [move(whole, device((x + e) % 4, y, z, c)) for e in (2, 1, 3)]
+                    self.spreads[d] += [move(whole, device((x + e) % 4, y, z, c), sem) for e in (2, 1, 3)]
                 else:
                     part = columns // 2
-                    spread = [
-                        move(block(source, first, count, column, part), device(x, y, (z + 2) % NZ, c)),
-                        move(block(source, first, count, column + part, part), device(x, y, (z + NZ - 2) % NZ, c)),
-                        move(whole, device(x, y, (z + 1) % NZ, c)),
-                        move(whole, device(x, y, (z + NZ - 1) % NZ, c)),
+                    self.spreads[d] += [
+                        move(block(source, first, count, column, part), device(x, y, (z + 2) % NZ, c), sem),
+                        move(block(source, first, count, column + part, part), device(x, y, (z + NZ - 2) % NZ, c), sem),
+                        move(whole, device(x, y, (z + 1) % NZ, c), sem),
+                        move(whole, device(x, y, (z + NZ - 1) % NZ, c), sem),
                     ]
-                self.spreads[d].append(spread)
-        self.late = {d: move(block((y + 4 - d) % 4, direct, ROWS - direct), other) for d in (1, 3, 2)}
+            self.late[d] = move(block(source, direct, ROWS - direct), other, self.core)
+
+    def received(self, rows, sem):
+        await_received(self.wall.at[:rows], sem, self.other)
 
     def fetch(self):
-        for fetched, _ in self.near:
-            fetched.start()
+        start_all(self.fetched[1] + self.fetched[3])
 
     def start(self):
         start_all(self.first)
@@ -146,22 +170,18 @@
         self.own.start()
 
     def spread(self):
-        for (fetched, passed), spread in zip(self.near, self.spreads[1] + self.spreads[3]):
-            fetched.wait_recv()
-            passed.start()
-            start_all(spread)
+        for d in (1, 3):
+            self.received(self.block_rows, self.near[d])
+            start_all(self.passed[d])
+            start_all(self.spreads[d])
 
     def across(self):
-        kinds = len(self.spreads[2])
-        for i, spread in enumerate(self.spreads[2]):
-            self.near[i][1].wait_recv()
-            self.near[kinds + i][1].wait_recv()
-            start_all(spread)
+        self.received(self.block_rows, self.far)
+        start_all(self.spreads[2])
 
     def collect(self):
         for d, late in self.late.items():
-            for copy in sum(self.spreads[d], []):
-                copy.wait_recv()
+            self.received(3 * self.block_rows, self.spread_sem[d])
             late.start()
 
     def forward(self):
@@ -177,38 +197,32 @@
 
     def arrived(self):
         self.own.wait()
-        for copy in [self.to_core] + self.cores + self.halves + list(self.late.values()):
-            copy.wait_recv()
+        self.received(4 * ROWS, self.core)
 
     def sent(self):
-        copies = [self.to_core] + self.first + self.forwards + self.cores + self.halves
-        copies += list(self.late.values()) + sum(sum(self.spreads.values(), []), [])
-        for fetched, passed in self.near:
-            copies += [fetched, passed]
-        for copy in copies:
-            copy.wait_send()
+        await_sent(self.wall.at[: self.rows_sent], self.send, self.other)
 
 
 class Ring:
-    def __init__(self, own, view, half, me, towards, other, send, recv):
+    def __init__(self, own, cots, view, half, me, towards, other, new):
         ahead, behind, across = (me + 1) % 4, (me + 3) % 4, (me + 2) % 4
+        self.cots, self.other = cots, other
+        self.send = send = new()
+        self.core = core = new()
         self.first = [
-            remote(own, view(me), send.at[0], recv.at[0], towards(ahead)),
-            remote(own, view(me), send.at[1], recv.at[1], towards(behind)),
-            remote(own, view(me), send.at[4], recv.at[4], other),
+            remote(own, view(me), send, new(), towards(ahead)),
+            remote(own, view(me), send, new(), towards(behind)),
+            remote(own, view(me), send, core, other),
         ]
         self.behind = [
-            remote(half(behind, 0), half(behind, 0), send.at[2], recv.at[2], towards(ahead)),
-            remote(view(behind), view(behind), send.at[5], recv.at[5], other),
+            remote(half(behind, 0), half(behind, 0), send, new(), towards(ahead)),
+            remote(view(behind), view(behind), send, core, other),
         ]
         self.ahead = [
-            remote(half(ahead, 1), half(ahead, 1), send.at[3], recv.at[3], towards(behind)),
-            remote(view(ahead), view(ahead), send.at[6], recv.at[6], other),
+            remote(half(ahead, 1), half(ahead, 1), send, new(), towards(behind)),
+            remote(view(ahead), view(ahead), send, core, other),
         ]
-        self.across = [
-            remote(half(across, 0), half(across, 0), send.at[7], recv.at[7], other),
-            remote(half(across, 1), half(across, 1), send.at[8], recv.at[8], other),
-        ]
+        self.across = [remote(half(across, h), half(across, h), send, core, other) for h in range(2)]
 
     def start(self):
         start_all(self.first)
@@ -226,16 +240,14 @@
         self.across[1].start()
 
     def arrived(self):
-        for copy in [self.first[2], self.behind[1], self.ahead[1]] + self.across:
-            copy.wait_recv()
+        await_received(self.cots.at[: 4 * ROWS], self.core, self.other)
 
     def sent(self):
-        for copy in self.first + self.behind + self.ahead + self.across:
-            copy.wait_send()
+        await_sent(self.cots.at[: 7 * ROWS], self.send, self.other)
 
 
 class Swap:
-    def __init__(self, held, landed, at, order, mask, send, recv):
+    def __init__(self, held, landed, at, order, mask, send, new):
         x, y, z, c = at
         self.held, self.landed, self.order, self.mask = held, landed, order, mask
         self.copies = []
@@ -243,7 +255,7 @@
             size = 1 << bit
             to = z + size - 2 * size * (z // size % 2)
             self.copies.append(
-                remote(held.at[step], landed.at[step], send.at[step], recv.at[step], device(x, y, to, c))
+                remote(held.at[step], landed.at[step], send, new(), device(x, y, to, c))
             )
 
     def start(self):
@@ -257,21 +269,16 @@
         if step < 2:
             self.copies[step + 1].start()
 
-    def sent(self):
-        for copy in self.copies:
-            copy.wait_send()
-
 
 def layer_kernel(
     mask_hbm, lengths_hbm, actions_hbm, gain_hbm, w_in_ref, w_out_ref, cot_hbm,
-    output_hbm, grad_hbm, weight_hbm,
-    mask_ref, lengths_ref, output, grad_input, weight_grad, store_sem,
+    output, grad_input, weight_grad,
+    mask_ref, lengths_ref,
     actions, gain, cot, wall, cots, cot_t, normed, normed_in, inverse_in,
     active, slopes, weights, score_slopes, attended, normed_out, inverse_out, mixed,
     far_normed, far_active, grad_att, grad_mix, grad_hidden,
     held, landed, all_mixed, total, sums, xbuf, part, zbuf, final, wide,
-    load_sem, wsend, wrecv, wlocal, csend, crecv, clocal, ssend, srecv,
-    msend, mrecv, xsend, xrecv, zsend, zrecv, asend, arecv,
+    sems,
 ):
     dp = lax.axis_index("dp")
     me = lax.axis_index("fsdp")
@@ -284,12 +291,18 @@
     in_z = [device(x, y, (z + d) % NZ, c) for d in range(1, NZ)]
     peers = in_group + in_x + in_z
 
+    used = [0]
+
+    def new():
+        used[0] += 1
+        return sems.at[used[0] - 1]
+
     loads = [
-        pltpu.make_async_copy(actions_hbm.at[0], actions, load_sem.at[0]),
-        pltpu.make_async_copy(cot_hbm.at[0], cot, load_sem.at[1]),
-        pltpu.make_async_copy(gain_hbm, gain, load_sem.at[2]),
-        pltpu.make_async_copy(mask_hbm, mask_ref, load_sem.at[3]),
-        pltpu.make_async_copy(lengths_hbm, lengths_ref, load_sem.at[4]),
+        pltpu.make_async_copy(actions_hbm.at[0], actions, new()),
+        pltpu.make_async_copy(cot_hbm.at[0], cot, new()),
+        pltpu.make_async_copy(gain_hbm, gain, new()),
+        pltpu.make_async_copy(mask_hbm, mask_ref, new()),
+        pltpu.make_async_copy(lengths_hbm, lengths_ref, new()),
     ]
     start_all(loads)
     barrier = pltpu.get_barrier_semaphore()
@@ -299,20 +312,21 @@
     sections = {
         t: Section(
             w_out_ref if t == OUT else w_in_ref.at[:, t * WIDTH : (t + 1) * WIDTH],
-            wall, t, at, wsend.at[t], wrecv.at[t], wlocal.at[t],
+            wall, t, at, new,
         )
         for t in range(5)
     }
     column = lambda i: pl.ds(pl.multiple_of((2 * i + c) * ROWS, ROWS), ROWS)
     cring = Ring(
-        cot_t,
+        cot_t, cots,
         lambda i: cots.at[:, column(i)],
         lambda i, h: cots.at[h * 512 : h * 512 + 512, column(i)],
-        y, lambda i: device(x, i, z, c), other, csend, crecv,
+        y, lambda i: device(x, i, z, c), other, new,
     )
-    cown = pltpu.make_async_copy(cot_t, cots.at[:, column(y)], clocal)
+    cown = pltpu.make_async_copy(cot_t, cots.at[:, column(y)], new())
     orders = [(2, 1, 0), (0, 1, 2), (2, 1, 0), (0, 1, 2)]
-    swaps = [Swap(held.at[i], landed.at[i], at, orders[i], mask_ref, ssend.at[i], srecv.at[i]) for i in range(4)]
+    swap_send = new()
+    swaps = [Swap(held.at[i], landed.at[i], at, orders[i], mask_ref, swap_send, new) for i in range(4)]
 
     pl.semaphore_wait(barrier, len(peers))
     sections[QUERIES].fetch()
@@ -347,12 +361,14 @@
     begin = jnp.where(row >= LAST, LAST, begin)
     visible = (col >= begin) & (col <= row)
 
-    def project(t):
+    def project(t, count=ROWS):
         for l in range(0, WIDTH, LANES):
-            hidden = dot(normed[...], wall[t, :, l : l + LANES])
+            hidden = dot(normed[:count], wall[t, :, l : l + LANES])
             value, slope = silu_parts(hidden)
-            active[t, :, l : l + LANES] = value.astype(BF16)
-            slopes[t, :, l : l + LANES] = slope
+            active[t, :, l : l + LANES] = value[:ROWS].astype(BF16)
+            slopes[t, :, l : l + LANES] = slope[:ROWS]
+            if count > ROWS:
+                far_active[t, :MOST, l : l + LANES] = value[ROWS:].astype(BF16)
 
     def small(t, rows, first, count):
         for l in range(0, WIDTH, LANES):
@@ -386,8 +402,6 @@
     sections[KEYS].collect()
     sections[QUERIES].finish()
     sections[VALUES].collect()
-    sections[KEYS].arrived()
-    project(KEYS)
     sections[QUERIES].arrived()
     project(QUERIES)
     swaps[0].turn(2)
@@ -395,14 +409,13 @@
     swaps[2].start()
     swaps[3].start()
     far_inputs = jnp.concatenate([held[0, 3], held[1, 3]], axis=0).astype(F32)
-    far_normed[:MOST] = (normalize(far_inputs)[0] * gain[...]).astype(BF16)
-    small(KEYS, far_normed[:MOST], 0, MOST)
+    normed[ROWS:] = (normalize(far_inputs)[0] * gain[...]).astype(BF16)
+    sections[KEYS].arrived()
+    project(KEYS, ROWS + MOST)
     sections[GATES].finish()
     sections[VALUES].arrived()
-    project(VALUES)
-    small(VALUES, far_normed[:MOST], 0, MOST)
+    project(VALUES, ROWS + MOST)
     sections[GATES].collect()
-    cring.forward()
 
     far_slopes = []
     for h in range(HEADS):
@@ -418,6 +431,7 @@
         attended[:LAST, head(h)] = local_part[:LAST]
         attended[LAST:, head(h)] = local_part[LAST:] + far_part
 
+    cring.forward()
     sections[GATES].arrived()
     project(GATES)
     for r in range(0, ROWS, CHUNK):
@@ -428,9 +442,8 @@
         for h in range(HEADS):
             mixed[h, r : r + CHUNK] = mix[:, head(h)]
     own_rows = pl.ds(pl.multiple_of(me * ROWS, ROWS), ROWS)
-    spread = [
-        remote(mixed.at[group[d]], all_mixed.at[own_rows], msend.at[d], mrecv.at[d], in_group[d]) for d in range(7)
-    ]
+    msend, mrecv, xsend, xrecv, zsend, zrecv, asend, arecv = [new() for _ in range(8)]
+    spread = [remote(mixed.at[group[d]], all_mixed.at[own_rows], msend, mrecv, in_group[d]) for d in range(7)]
     start_all(spread)
     all_mixed[own_rows] = mixed[me]
     swaps[3].turn(0)
@@ -441,19 +454,16 @@
     swaps[3].turn(1)
     swaps[2].turn(1)
 
-    for copy in spread:
-        copy.wait_recv()
+    await_received(all_mixed.at[: 7 * ROWS], mrecv, other)
     cown.wait()
     cring.arrived()
-    xcopies = []
     for d in (2, 1, 3, 0):
         quarter = pl.ds(pl.multiple_of((x + d) % 4 * 256, 256), 256)
         product = dot(cots[quarter], all_mixed[...])
         if d:
             sums[quarter] = product.astype(BF16)
-            copy = remote(sums.at[quarter], xbuf.at[d - 1], xsend.at[d - 1], xrecv.at[d - 1], in_x[d - 1])
+            copy = remote(sums.at[quarter], xbuf.at[d - 1], xsend, xrecv, in_x[d - 1])
             copy.start()
-            xcopies.append(copy)
         else:
             total[...] = product
 
@@ -461,9 +471,9 @@
     swaps[2].turn(2)
     swaps[3].turn(2)
     spill_inputs = held[2, 3].astype(F32)
-    far_normed[MOST:] = (normalize(spill_inputs)[0] * gain[...]).astype(BF16)
+    far_normed[...] = (normalize(spill_inputs)[0] * gain[...]).astype(BF16)
     for t in (GATES, VALUES, QUERIES, KEYS):
-        small(t, far_normed[MOST:], MOST, SPILL)
+        small(t, far_normed[...], MOST, SPILL)
     rows16 = lax.broadcasted_iota(jnp.int32, (SPILL, SPILL), 0)
     cols16 = lax.broadcasted_iota(jnp.int32, (SPILL, SPILL), 1)
     causal = cols16 <= rows16
@@ -479,13 +489,12 @@
         near_attended.append(
             dot(weight, active[VALUES, FIRST:LAST, head(h)]) + dot(weight2, far_active[VALUES, MOST:, head(h)])
         )
-    for copy in xcopies:
-        copy.wait_recv()
+    await_received(xbuf, xrecv, other)
     part[...] = (
         total[...] + xbuf[0].astype(F32) + xbuf[1].astype(F32) + xbuf[2].astype(F32)
     ).astype(BF16)
     zcopies = [
-        remote(part.at[pl.ds(pl.multiple_of((z + d + 1) % NZ * 16, 16), 16)], zbuf.at[d], zsend.at[d], zrecv.at[d], in_z[d])
+        remote(part.at[pl.ds(pl.multiple_of((z + d + 1) % NZ * 16, 16), 16)], zbuf.at[d], zsend, zrecv, in_z[d])
         for d in range(NZ - 1)
     ]
     for d in (7, 6, 8, 5, 9, 4, 10, 3, 11, 2, 12, 1, 13, 0, 14):
@@ -507,15 +516,9 @@
 
     mixed_rows = jnp.concatenate([mixed[h] for h in range(HEADS)], axis=1)
     for l in range(0, WIDTH, LANES):
-        output[:, l : l + LANES] = (
+        output[0, :, l : l + LANES] = (
             dot(mixed_rows, wall[OUT, :, l : l + LANES]) + actions[:, l : l + LANES].astype(F32)
         ).astype(BF16)
-    stores = [
-        pltpu.make_async_copy(output, output_hbm.at[0], store_sem.at[0]),
-        pltpu.make_async_copy(grad_input, grad_hbm.at[0], store_sem.at[1]),
-        pltpu.make_async_copy(weight_grad, weight_hbm, store_sem.at[2]),
-    ]
-    stores[0].start()
     near_grad = dot_nt(held[3, 3], wall[OUT])
     near_normed, near_inverse = normalize(jnp.concatenate(near_attended, axis=1))
     near_att = norm_backward(
@@ -544,13 +547,12 @@
             grad_hidden[t, FIRST:LAST, head(h)] = ((grad[FIRST:LAST] + extra) * slope[FIRST:LAST]).astype(BF16)
             grad_hidden[t, LAST:, head(h)] = (grad[LAST:] * slope[LAST:]).astype(BF16)
 
-    for copy in zcopies:
-        copy.wait_recv()
+    await_received(zbuf, zrecv, other)
     summed = part[pl.ds(pl.multiple_of(z * 16, 16), 16)].astype(F32)
     for d in range(NZ - 1):
         summed = summed + zbuf[d].astype(F32)
     final[...] = summed * (1.0 / 256.0)
-    acopies = [remote(final, wide.at[me], asend.at[d], arecv.at[d], in_group[d]) for d in range(7)]
+    acopies = [remote(final, wide.at[me], asend, arecv, in_group[d]) for d in range(7)]
     start_all(acopies)
     wide[me] = final[...]
 
@@ -563,43 +565,33 @@
         ) * gain[:, l : l + LANES]
     for r in range(0, ROWS, CHUNK):
         span = slice(r, r + CHUNK)
-        grad_input[span] = (
+        grad_input[0, span] = (
             cot[span].astype(F32) + norm_backward(grad_mix[span], normed_in[span], inverse_in[span])
         ).astype(BF16)
 
-    stores[1].start()
     for section in sections.values():
         section.sent()
     cring.sent()
-    for swap in swaps:
-        swap.sent()
-    for copy in spread + xcopies + zcopies:
-        copy.wait_send()
-    for copy in acopies:
-        copy.wait_recv()
+    await_sent(wall.at[OUT, : 12 * SPILL], swap_send, other)
+    await_sent(all_mixed.at[: 7 * ROWS], msend, other)
+    await_sent(xbuf, xsend, other)
+    await_sent(zbuf, zsend, other)
+    await_received(wide.at[:7], arecv, other)
     for i in range(8):
         weight_grad[:, i * 128 : (i + 1) * 128] = wide[i]
-    stores[2].start()
-    for copy in acopies:
-        copy.wait_send()
-    for copy in stores:
+    await_sent(wide.at[:7], asend, other)
+
+
+def publish_kernel(*refs):
+    copies = [pltpu.make_async_copy(refs[i], refs[3 + i], refs[6].at[i]) for i in range(3)]
+    start_all(copies)
+    for copy in copies:
         copy.wait()
 
 
-def publish_kernel(*refs):
-    sources, results, staged, load_sem, store_sem = refs[:3], refs[3:6], refs[6:9], refs[9], refs[10]
-    loads = [pltpu.make_async_copy(sources[i], staged[i], load_sem.at[i]) for i in range(3)]
-    stores = [pltpu.make_async_copy(staged[i], results[i], store_sem.at[i]) for i in range(3)]
-    start_all(loads)
-    for load, store in zip(loads, stores):
-        load.wait()
-        store.start()
-    for store in stores:
-        store.wait()
-
-
 def per_device(actions, lengths, partner_mask, norm_gain, w_in, w_out, cotangent):
-    hbm = pl.BlockSpec(memory_space=pl.ANY)
+    hbm = pl.BlockSpec(memory_space=pltpu.HBM)
+    vmem = pl.BlockSpec(memory_space=pltpu.VMEM)
     dma = pltpu.SemaphoreType.DMA
     block = (ROWS, WIDTH)
     shapes = (
@@ -609,23 +601,20 @@
     )
     results = pl.pallas_call(
         layer_kernel,
-        out_shape=shapes,
+        out_shape=tuple(pltpu.VMEM(shape.shape, shape.dtype) for shape in shapes),
         in_specs=[hbm] * 7,
-        out_specs=(hbm, hbm, hbm),
+        out_specs=(vmem, vmem, vmem),
         scratch_shapes=[
             pltpu.SMEM((1, 1), jnp.int32),
             pltpu.SMEM((1, 1, 7), jnp.int32),
-            pltpu.VMEM(block, BF16),
-            pltpu.VMEM(block, BF16),
-            pltpu.VMEM((16, WIDTH), F32),
-            dma((3,)),
+
             pltpu.VMEM(block, BF16),
             pltpu.VMEM((1, WIDTH), F32),
             pltpu.VMEM(block, BF16),
             pltpu.VMEM((5, WIDTH, WIDTH), BF16),
             pltpu.VMEM((WIDTH, WIDTH), BF16),
             pltpu.VMEM((WIDTH, ROWS), BF16),
-            pltpu.VMEM(block, BF16),
+            pltpu.VMEM((ROWS + MOST, WIDTH), BF16),
             pltpu.VMEM(block, F32),
             pltpu.VMEM((ROWS, 1), F32),
             pltpu.VMEM((4, ROWS, WIDTH), BF16),
@@ -636,7 +625,7 @@
             pltpu.VMEM(block, F32),
             pltpu.VMEM((ROWS, 1), F32),
             pltpu.VMEM((HEADS, ROWS, HEAD_DIM), BF16),
-            pltpu.VMEM((MOST + SPILL, WIDTH), BF16),
+            pltpu.VMEM((SPILL, WIDTH), BF16),
             pltpu.VMEM((4, MOST + SPILL, WIDTH), BF16),
             pltpu.VMEM(block, BF16),
             pltpu.VMEM(block, F32),
@@ -651,9 +640,7 @@
             pltpu.VMEM((NZ - 1, 16, 128), BF16),
             pltpu.VMEM((16, 128), F32),
             pltpu.VMEM((8, 16, 128), F32),
-            dma((5,)), dma((5, 42)), dma((5, 42)), dma((5,)), dma((9,)), dma((9,)), dma,
-            dma((4, 3)), dma((4, 3)), dma((7,)), dma((7,)), dma((3,)), dma((3,)),
-            dma((NZ - 1,)), dma((NZ - 1,)), dma((7,)), dma((7,)),
+            dma((SEMAPHORES,)),
         ],
         compiler_params=pltpu.CompilerParams(
             collective_id=0, has_side_effects=True, vmem_limit_bytes=56 * 1024 * 1024
@@ -663,10 +650,10 @@
     return pl.pallas_call(
         publish_kernel,
         out_shape=shapes,
-        in_specs=[hbm, hbm, hbm],
+        in_specs=[vmem, vmem, vmem],
         out_specs=(hbm, hbm, hbm),
-        scratch_shapes=[pltpu.VMEM(shape.shape, shape.dtype) for shape in shapes] + [dma((3,)), dma((3,))],
-        compiler_params=pltpu.CompilerParams(vmem_limit_bytes=60 * 1024 * 1024),
+        scratch_shapes=[dma((3,))],
+        compiler_params=pltpu.CompilerParams(vmem_limit_bytes=16 * 1024 * 1024),
         name="publish",
     )(*results)
 

time: 74.9 us -> 70 us (0.935)
  Pallas kernels: 73.5 us -> 68.6 us
    pallas_call x2, Pallas kernels: 73.5 us -> 68.6 us  [the longest x1 67.8 us: per_device(): pl.pallas_call(layer_kernel, out_shape=tuple((pltpu.VMEM(shape.shape, sha...]
where the time goes in v4:
time: 70 us; the launch traced here: 69.9 us
  Pallas kernels  68.6 us (98%)
  between operations  1.29 us (2%)
    pallas_call x1, Pallas kernels, per_device(): pl.pallas_call(layer_kernel, out_shape=tuple((pltpu.VMEM(shape.shape, sha...  67.8 us

profile of v4, /device:TPU:1, one launch (start us, length us, event | category | flops | bytes accessed | tf_op | source)
XLA Modules:
  0.0 69.9 jit_solution(1646275962916865472)
XLA Ops:
  1.3 67.8 %layer.1 = (bf16[1,128,1024]{2,1,0:T(8,128)(2,1)S(1)}, bf16[1,128,1024]{2,1,0:T(8,128)(2,1)S(1)}, f32[16,1024]{1,0:T(8,128)S(1)}) custom-call(s32[1,1]{1,0:T(1,128)S(6)} %copy.10.mask_hbm, s32[1,1,7]{2,1,0:T(1,128)} %lengths_hbm.1, bf16[1,128,1024]{2,1,0:T(8,128)(2,1)} %actions_hbm.1, f32[1,1024]{1,0:T(1,128)} %bitcast.1, bf16[128,4096]{1,0:T(8,128)(2,1)} %w_in_ref.1, ...), custom_call_target="tpu_custom_call" | custom-call | tf_op jit(solution)/shard_map/layer/pallas_call | solution.py:602
  69.0 0.8 %publish.1 = (bf16[1,128,1024]{2,1,0:T(8,128)(2,1)}, bf16[1,128,1024]{2,1,0:T(8,128)(2,1)}, f32[16,1024]{1,0:T(8,128)}) custom-call(bf16[1,128,1024]{2,1,0:T(8,128)(2,1)S(1)} %get-tuple-element.6.refs_0_, bf16[1,128,1024]{2,1,0:T(8,128)(2,1)S(1)} %get-tuple-element.7.refs_1_, f32[16,1024]{1,0:T(8,128)S(1)} %get-tuple-element.8.refs_2_), custom_call_target="tpu_custom_call" | custom-call | tf_op jit(solution)/shard_map/publish/pallas_call | solution.py:650

commit v5 on v4

--- a/solution.py
+++ b/solution.py
@@ -23,13 +23,13 @@
 GATES, VALUES, QUERIES, KEYS, OUT = range(5)
 HALF = WIDTH // 2
 PLAN = {
-    QUERIES: (64, [("x", 64, 16, 0, WIDTH)]),
+    QUERIES: (128, []),
     KEYS: (0, [("x", 0, 16, 0, WIDTH), ("z", 64, 16, 0, WIDTH)]),
     VALUES: (0, [("x", 0, 16, 0, WIDTH), ("z", 64, 16, 0, WIDTH)]),
     GATES: (64, [("x", 64, 16, 0, HALF), ("z", 64, 16, HALF, HALF)]),
-    OUT: (0, [("x", 0, 16, 0, WIDTH), ("z", 64, 16, 0, WIDTH)]),
+    OUT: (128, []),
 }
-SEMAPHORES = 86
+SEMAPHORES = 78
 CHUNK = 32
 LANES = 256
 
@@ -125,6 +125,8 @@
             ]
             self.halves = [move(block(across, h * half, half), other, self.core) for h in range(2)]
         self.fetched, self.passed, self.spreads, self.late = {}, {}, {}, {}
+        if not blocks:
+            return
         self.near, self.far, self.spread_sem = {1: new(), 3: new()}, new(), {d: new() for d in (1, 3, 2)}
         self.block_rows = sum(count * columns // WIDTH for _, _, count, _, columns in blocks)
         for d, source, to in ((1, behind, to_ahead), (3, ahead, to_behind)):
@@ -169,11 +171,13 @@
         self.to_core.start()
         self.own.start()
 
-    def spread(self):
+    def pass_on(self):
         for d in (1, 3):
             self.received(self.block_rows, self.near[d])
             start_all(self.passed[d])
-            start_all(self.spreads[d])
+
+    def spread(self):
+        start_all(self.spreads[1] + self.spreads[3])
 
     def across(self):
         self.received(self.block_rows, self.far)
@@ -277,19 +281,22 @@
     actions, gain, cot, wall, cots, cot_t, normed, normed_in, inverse_in,
     active, slopes, weights, score_slopes, attended, normed_out, inverse_out, mixed,
     far_normed, far_active, grad_att, grad_mix, grad_hidden,
-    held, landed, all_mixed, total, sums, xbuf, part, zbuf, final, wide,
+    held, landed, all_mixed, total, sums, ybuf, part, zbuf, final, wide,
     sems,
 ):
     dp = lax.axis_index("dp")
-    me = lax.axis_index("fsdp")
-    x, y, z, c = dp // NZ, me // 2, dp % NZ, me % 2
+    fsdp = lax.axis_index("fsdp")
+    x, y, z, c = dp // NZ, fsdp // 2, dp % NZ, fsdp % 2
+    me = 2 * x + c
     at = (x, y, z, c)
     other = device(x, y, z, 1 - c)
-    group = [(me + d) % 8 for d in range(1, 8)]
-    in_group = [(dp, i) for i in group]
-    in_x = [device((x + d) % 4, y, z, c) for d in range(1, 4)]
+    group = [(2 * x + c + d) % 8 for d in range(1, 8)]
+    in_group = [device(i // 2, y, z, i % 2) for i in group]
+    in_y = [device(x, (y + d) % 4, z, c) for d in range(1, 4)]
     in_z = [device(x, y, (z + d) % NZ, c) for d in range(1, NZ)]
-    peers = in_group + in_x + in_z
+    ends = [device(y, i // 2, z, i % 2) for i in range(8)]
+    begins = [device(i // 2, x, z, i % 2) for i in range(8)]
+    apart = [jnp.logical_or(x != y, i != me) for i in range(8)]
 
     used = [0]
 
@@ -304,10 +311,15 @@
         pltpu.make_async_copy(mask_hbm, mask_ref, new()),
         pltpu.make_async_copy(lengths_hbm, lengths_ref, new()),
     ]
+    barrier = pltpu.get_barrier_semaphore()
+    for target in [in_z[d] for d in (7, 6, 8, 5, 9, 4, 10, 3, 11, 2, 12, 1, 13, 0, 14)] + in_group + in_y:
+        pl.semaphore_signal(barrier, inc=1, device_id=target, device_id_type=MESH)
+    for i in range(8):
+        @pl.when(apart[i])
+        def _():
+            pl.semaphore_signal(barrier, inc=1, device_id=ends[i], device_id_type=MESH)
+            pl.semaphore_signal(barrier, inc=1, device_id=begins[i], device_id_type=MESH)
     start_all(loads)
-    barrier = pltpu.get_barrier_semaphore()
-    for target in peers:
-        pl.semaphore_signal(barrier, inc=1, device_id=target, device_id_type=MESH)
 
     sections = {
         t: Section(
@@ -321,15 +333,15 @@
         cot_t, cots,
         lambda i: cots.at[:, column(i)],
         lambda i, h: cots.at[h * 512 : h * 512 + 512, column(i)],
-        y, lambda i: device(x, i, z, c), other, new,
+        x, lambda i: device(i, y, z, c), other, new,
     )
-    cown = pltpu.make_async_copy(cot_t, cots.at[:, column(y)], new())
-    orders = [(2, 1, 0), (0, 1, 2), (2, 1, 0), (0, 1, 2)]
+    cown = pltpu.make_async_copy(cot_t, cots.at[:, column(x)], new())
+    orders = [(2, 1, 0), (0, 1, 2), (2, 1, 0), (1, 2, 0)]
     swap_send = new()
     swaps = [Swap(held.at[i], landed.at[i], at, orders[i], mask_ref, swap_send, new) for i in range(4)]
 
-    pl.semaphore_wait(barrier, len(peers))
-    sections[QUERIES].fetch()
+    pl.semaphore_wait(barrier, 41 - 2 * (x == y).astype(jnp.int32))
+    sections[KEYS].fetch()
     for copy in loads:
         copy.wait()
     held[0, 0] = actions[FIRST : FIRST + 16]
@@ -338,17 +350,19 @@
     held[3, 0] = cot[LAST:]
     swaps[0].start()
     swaps[1].start()
-    sections[KEYS].fetch()
     sections[VALUES].fetch()
     sections[GATES].fetch()
+    cot_t[...] = cot[...].astype(F32).T.astype(BF16)
+    cring.start()
+    cown.start()
+    sections[KEYS].start()
+    sections[VALUES].start()
 
     for r in range(0, ROWS, CHUNK):
         n, inverse = normalize(actions[r : r + CHUNK].astype(F32))
         normed_in[r : r + CHUNK] = n
         inverse_in[r : r + CHUNK] = inverse
         normed[r : r + CHUNK] = (n * gain[...]).astype(BF16)
-    cot_t[...] = cot[...].astype(F32).T.astype(BF16)
-    cown.start()
 
     row = lax.broadcasted_iota(jnp.int32, (ROWS, ROWS), 0)
     col = lax.broadcasted_iota(jnp.int32, (ROWS, ROWS), 1)
@@ -378,44 +392,42 @@
     def head(h):
         return slice(h * HEAD_DIM, (h + 1) * HEAD_DIM)
 
-    sections[QUERIES].spread()
+    swaps[1].turn(0)
+    sections[KEYS].pass_on()
+    sections[QUERIES].start()
     sections[KEYS].spread()
-    sections[KEYS].start()
-    sections[VALUES].start()
-    swaps[1].turn(0)
+    sections[VALUES].pass_on()
     sections[VALUES].spread()
-    sections[QUERIES].start()
-    sections[QUERIES].across()
+    sections[GATES].pass_on()
+    sections[GATES].start()
     swaps[0].turn(0)
+    swaps[1].turn(1)
     sections[KEYS].across()
     sections[GATES].spread()
-    sections[GATES].start()
     sections[VALUES].across()
     sections[GATES].across()
-    swaps[1].turn(1)
+    cring.forward()
     sections[QUERIES].forward()
     swaps[0].turn(1)
+    sections[KEYS].collect()
     sections[GATES].forward()
-    cring.start()
-    sections[OUT].fetch()
-    sections[QUERIES].collect()
-    sections[KEYS].collect()
-    sections[QUERIES].finish()
+    sections[OUT].start()
     sections[VALUES].collect()
-    sections[QUERIES].arrived()
-    project(QUERIES)
+    swaps[2].start()
+    swaps[3].start()
     swaps[0].turn(2)
     swaps[1].turn(2)
-    swaps[2].start()
-    swaps[3].start()
     far_inputs = jnp.concatenate([held[0, 3], held[1, 3]], axis=0).astype(F32)
     normed[ROWS:] = (normalize(far_inputs)[0] * gain[...]).astype(BF16)
     sections[KEYS].arrived()
     project(KEYS, ROWS + MOST)
-    sections[GATES].finish()
+    sections[QUERIES].finish()
     sections[VALUES].arrived()
     project(VALUES, ROWS + MOST)
     sections[GATES].collect()
+    sections[GATES].finish()
+    sections[QUERIES].arrived()
+    project(QUERIES)
 
     far_slopes = []
     for h in range(HEADS):
@@ -431,7 +443,6 @@
         attended[:LAST, head(h)] = local_part[:LAST]
         attended[LAST:, head(h)] = local_part[LAST:] + far_part
 
-    cring.forward()
     sections[GATES].arrived()
     project(GATES)
     for r in range(0, ROWS, CHUNK):
@@ -442,32 +453,60 @@
         for h in range(HEADS):
             mixed[h, r : r + CHUNK] = mix[:, head(h)]
     own_rows = pl.ds(pl.multiple_of(me * ROWS, ROWS), ROWS)
-    msend, mrecv, xsend, xrecv, zsend, zrecv, asend, arecv = [new() for _ in range(8)]
+    msend, mrecv, ysend, yrecv, zsend, zrecv, asend, arecv = [new() for _ in range(8)]
     spread = [remote(mixed.at[group[d]], all_mixed.at[own_rows], msend, mrecv, in_group[d]) for d in range(7)]
     start_all(spread)
     all_mixed[own_rows] = mixed[me]
+    cring.finish()
+    sections[OUT].forward()
+    swaps[2].turn(0)
     swaps[3].turn(0)
-    swaps[2].turn(0)
-    sections[OUT].spread()
-    sections[OUT].start()
-    cring.finish()
-    swaps[3].turn(1)
-    swaps[2].turn(1)
 
     await_received(all_mixed.at[: 7 * ROWS], mrecv, other)
     cown.wait()
     cring.arrived()
     for d in (2, 1, 3, 0):
-        quarter = pl.ds(pl.multiple_of((x + d) % 4 * 256, 256), 256)
+        quarter = pl.ds(pl.multiple_of((y + d) % 4 * 256, 256), 256)
         product = dot(cots[quarter], all_mixed[...])
         if d:
             sums[quarter] = product.astype(BF16)
-            copy = remote(sums.at[quarter], xbuf.at[d - 1], xsend, xrecv, in_x[d - 1])
+            copy = remote(sums.at[quarter], ybuf.at[d - 1], ysend, yrecv, in_y[d - 1])
             copy.start()
         else:
             total[...] = product
 
-    sections[OUT].across()
+    swaps[2].turn(1)
+    swaps[3].turn(1)
+    sections[OUT].finish()
+    sections[OUT].arrived()
+    for l in range(0, WIDTH, LANES):
+        grad_mix[:, l : l + LANES] = dot_nt(cot[...], wall[OUT, l : l + LANES])
+
+    for r in range(0, ROWS, CHUNK):
+        span = slice(r, r + CHUNK)
+        grad = grad_mix[span]
+        n = normed_out[span]
+        grad_hidden[GATES, span] = (grad * n * slopes[GATES, span]).astype(BF16)
+        grad_att[span] = norm_backward(
+            grad * active[GATES, span].astype(F32), n, inverse_out[span]
+        ).astype(BF16)
+
+    mixed_rows = jnp.concatenate([mixed[h] for h in range(HEADS)], axis=1)
+    for l in range(0, WIDTH, LANES):
+        output[0, :, l : l + LANES] = (
+            dot(mixed_rows, wall[OUT, :, l : l + LANES]) + actions[:, l : l + LANES].astype(F32)
+        ).astype(BF16)
+    await_received(ybuf, yrecv, other)
+    part[...] = (
+        total[...] + ybuf[0].astype(F32) + ybuf[1].astype(F32) + ybuf[2].astype(F32)
+    ).astype(BF16)
+    zcopies = [
+        remote(part.at[pl.ds(pl.multiple_of((z + d + 1) % NZ * 16, 16), 16)], zbuf.at[d], zsend, zrecv, in_z[d])
+        for d in range(NZ - 1)
+    ]
+    for d in (7, 6, 8, 5, 9, 4, 10, 3, 11, 2, 12, 1, 13, 0, 14):
+        zcopies[d].start()
+
     swaps[2].turn(2)
     swaps[3].turn(2)
     spill_inputs = held[2, 3].astype(F32)
@@ -489,36 +528,6 @@
         near_attended.append(
             dot(weight, active[VALUES, FIRST:LAST, head(h)]) + dot(weight2, far_active[VALUES, MOST:, head(h)])
         )
-    await_received(xbuf, xrecv, other)
-    part[...] = (
-        total[...] + xbuf[0].astype(F32) + xbuf[1].astype(F32) + xbuf[2].astype(F32)
-    ).astype(BF16)
-    zcopies = [
-        remote(part.at[pl.ds(pl.multiple_of((z + d + 1) % NZ * 16, 16), 16)], zbuf.at[d], zsend, zrecv, in_z[d])
-        for d in range(NZ - 1)
-    ]
-    for d in (7, 6, 8, 5, 9, 4, 10, 3, 11, 2, 12, 1, 13, 0, 14):
-        zcopies[d].start()
-
-    sections[OUT].collect()
-    sections[OUT].arrived()
-    for l in range(0, WIDTH, LANES):
-        grad_mix[:, l : l + LANES] = dot_nt(cot[...], wall[OUT, l : l + LANES])
-
-    for r in range(0, ROWS, CHUNK):
-        span = slice(r, r + CHUNK)
-        grad = grad_mix[span]
-        n = normed_out[span]
-        grad_hidden[GATES, span] = (grad * n * slopes[GATES, span]).astype(BF16)
-        grad_att[span] = norm_backward(
-            grad * active[GATES, span].astype(F32), n, inverse_out[span]
-        ).astype(BF16)
-
-    mixed_rows = jnp.concatenate([mixed[h] for h in range(HEADS)], axis=1)
-    for l in range(0, WIDTH, LANES):
-        output[0, :, l : l + LANES] = (
-            dot(mixed_rows, wall[OUT, :, l : l + LANES]) + actions[:, l : l + LANES].astype(F32)
-        ).astype(BF16)
     near_grad = dot_nt(held[3, 3], wall[OUT])
     near_normed, near_inverse = normalize(jnp.concatenate(near_attended, axis=1))
     near_att = norm_backward(
@@ -552,9 +561,17 @@
     for d in range(NZ - 1):
         summed = summed + zbuf[d].astype(F32)
     final[...] = summed * (1.0 / 256.0)
-    acopies = [remote(final, wide.at[me], asend, arecv, in_group[d]) for d in range(7)]
-    start_all(acopies)
-    wide[me] = final[...]
+    for i in range(8):
+        copy = remote(final, wide.at[me], asend, arecv, ends[i])
+
+        @pl.when(apart[i])
+        def _():
+            copy.start()
+
+    @pl.when(x == y)
+    def _():
+        wide[me] = final[...]
+
 
     for l in range(0, WIDTH, LANES):
         grad_mix[:, l : l + LANES] = (
@@ -574,12 +591,26 @@
     cring.sent()
     await_sent(wall.at[OUT, : 12 * SPILL], swap_send, other)
     await_sent(all_mixed.at[: 7 * ROWS], msend, other)
-    await_sent(xbuf, xsend, other)
+    await_sent(ybuf, ysend, other)
     await_sent(zbuf, zsend, other)
-    await_received(wide.at[:7], arecv, other)
+    @pl.when(x == y)
+    def _():
+        await_received(wide.at[:7], arecv, other)
+
+    @pl.when(x != y)
+    def _():
+        await_received(wide, arecv, other)
+
     for i in range(8):
         weight_grad[:, i * 128 : (i + 1) * 128] = wide[i]
-    await_sent(wide.at[:7], asend, other)
+
+    @pl.when(x == y)
+    def _():
+        await_sent(wide.at[:7], asend, other)
+
+    @pl.when(x != y)
+    def _():
+        await_sent(wide, asend, other)
 
 
 def publish_kernel(*refs):

time: 70 us -> 66.9 us (0.956)
  Pallas kernels: 68.6 us -> 65.5 us
    pallas_call x1, Pallas kernels: 67.8 us -> 64.7 us  [per_device(): pl.pallas_call(layer_kernel, out_shape=tuple((pltpu.VMEM(shape.shape, sha...]
where the time goes in v5:
time: 66.9 us; the launch traced here: 66.8 us
  Pallas kernels  65.5 us (98%)
  between operations  1.29 us (2%)
    pallas_call x1, Pallas kernels, per_device(): pl.pallas_call(layer_kernel, out_shape=tuple((pltpu.VMEM(shape.shape, sha...  64.7 us

profile of v5, /device:TPU:1, one launch (start us, length us, event | category | flops | bytes accessed | tf_op | source)
XLA Modules:
  0.0 66.8 jit_solution(17464628971324437172)
XLA Ops:
  1.3 64.7 %layer.1 = (bf16[1,128,1024]{2,1,0:T(8,128)(2,1)S(1)}, bf16[1,128,1024]{2,1,0:T(8,128)(2,1)S(1)}, f32[16,1024]{1,0:T(8,128)S(1)}) custom-call(s32[1,1]{1,0:T(1,128)S(6)} %copy.10.mask_hbm, s32[1,1,7]{2,1,0:T(1,128)} %lengths_hbm.1, bf16[1,128,1024]{2,1,0:T(8,128)(2,1)} %actions_hbm.1, f32[1,1024]{1,0:T(1,128)} %bitcast.1, bf16[128,4096]{1,0:T(8,128)(2,1)} %w_in_ref.1, ...), custom_call_target="tpu_custom_call" | custom-call | tf_op jit(solution)/shard_map/layer/pallas_call | solution.py:633
  66.0 0.8 %publish.1 = (bf16[1,128,1024]{2,1,0:T(8,128)(2,1)}, bf16[1,128,1024]{2,1,0:T(8,128)(2,1)}, f32[16,1024]{1,0:T(8,128)}) custom-call(bf16[1,128,1024]{2,1,0:T(8,128)(2,1)S(1)} %get-tuple-element.6.refs_0_, bf16[1,128,1024]{2,1,0:T(8,128)(2,1)S(1)} %get-tuple-element.7.refs_1_, f32[16,1024]{1,0:T(8,128)S(1)} %get-tuple-element.8.refs_2_), custom_call_target="tpu_custom_call" | custom-call | tf_op jit(solution)/shard_map/publish/pallas_call | solution.py:681

commit v6 on v5

--- a/solution.py
+++ b/solution.py
@@ -23,9 +23,9 @@
 GATES, VALUES, QUERIES, KEYS, OUT = range(5)
 HALF = WIDTH // 2
 PLAN = {
-    QUERIES: (128, []),
+    VALUES: (128, []),
     KEYS: (0, [("x", 0, 16, 0, WIDTH), ("z", 64, 16, 0, WIDTH)]),
-    VALUES: (0, [("x", 0, 16, 0, WIDTH), ("z", 64, 16, 0, WIDTH)]),
+    QUERIES: (0, [("x", 0, 16, 0, WIDTH), ("z", 64, 16, 0, WIDTH)]),
     GATES: (64, [("x", 64, 16, 0, HALF), ("z", 64, 16, HALF, HALF)]),
     OUT: (128, []),
 }
@@ -350,13 +350,13 @@
     held[3, 0] = cot[LAST:]
     swaps[0].start()
     swaps[1].start()
-    sections[VALUES].fetch()
+    sections[QUERIES].fetch()
     sections[GATES].fetch()
     cot_t[...] = cot[...].astype(F32).T.astype(BF16)
     cring.start()
     cown.start()
     sections[KEYS].start()
-    sections[VALUES].start()
+    sections[QUERIES].start()
 
     for r in range(0, ROWS, CHUNK):
         n, inverse = normalize(actions[r : r + CHUNK].astype(F32))
@@ -394,52 +394,53 @@
 
     swaps[1].turn(0)
     sections[KEYS].pass_on()
-    sections[QUERIES].start()
+    sections[VALUES].start()
     sections[KEYS].spread()
-    sections[VALUES].pass_on()
-    sections[VALUES].spread()
+    sections[QUERIES].pass_on()
+    sections[QUERIES].spread()
     sections[GATES].pass_on()
     sections[GATES].start()
     swaps[0].turn(0)
     swaps[1].turn(1)
     sections[KEYS].across()
     sections[GATES].spread()
-    sections[VALUES].across()
+    sections[QUERIES].across()
     sections[GATES].across()
     cring.forward()
-    sections[QUERIES].forward()
+    sections[VALUES].forward()
     swaps[0].turn(1)
     sections[KEYS].collect()
     sections[GATES].forward()
     sections[OUT].start()
-    sections[VALUES].collect()
+    sections[QUERIES].collect()
     swaps[2].start()
     swaps[3].start()
     swaps[0].turn(2)
     swaps[1].turn(2)
     far_inputs = jnp.concatenate([held[0, 3], held[1, 3]], axis=0).astype(F32)
     normed[ROWS:] = (normalize(far_inputs)[0] * gain[...]).astype(BF16)
+    sections[VALUES].finish()
     sections[KEYS].arrived()
     project(KEYS, ROWS + MOST)
-    sections[QUERIES].finish()
-    sections[VALUES].arrived()
-    project(VALUES, ROWS + MOST)
+    sections[QUERIES].arrived()
+    project(QUERIES)
     sections[GATES].collect()
     sections[GATES].finish()
-    sections[QUERIES].arrived()
-    project(QUERIES)
-
-    far_slopes = []
+
+    far_slopes, far_weights = [], []
     for h in range(HEADS):
-        q, k, v = active[QUERIES, :, head(h)], active[KEYS, :, head(h)], active[VALUES, :, head(h)]
+        q, k = active[QUERIES, :, head(h)], active[KEYS, :, head(h)]
         value, slope = silu_parts(dot_nt(q, k) * SCALE)
-        weight = (jnp.where(visible, value, 0.0) / MOST).astype(BF16)
-        weights[h] = weight
+        weights[h] = (jnp.where(visible, value, 0.0) / MOST).astype(BF16)
         score_slopes[h] = jnp.where(visible, slope, 0.0) * BACK
         value, slope = silu_parts(dot_nt(q[LAST:], far_active[KEYS, :MOST, head(h)]) * SCALE)
         far_slopes.append(slope * BACK)
-        far_part = dot((value / MOST).astype(BF16), far_active[VALUES, :MOST, head(h)])
-        local_part = dot(weight, v)
+        far_weights.append((value / MOST).astype(BF16))
+    sections[VALUES].arrived()
+    project(VALUES, ROWS + MOST)
+    for h in range(HEADS):
+        local_part = dot(weights[h], active[VALUES, :, head(h)])
+        far_part = dot(far_weights[h], far_active[VALUES, :MOST, head(h)])
         attended[:LAST, head(h)] = local_part[:LAST]
         attended[LAST:, head(h)] = local_part[LAST:] + far_part
 

time: 66.9 us -> 66.4 us (level)
  no operation moved by 1% of the time
where the time goes in v6:
time: 66.4 us; the launch traced here: 66.2 us
  Pallas kernels  65 us (98%)
  between operations  1.29 us (2%)
    pallas_call x1, Pallas kernels, per_device(): pl.pallas_call(layer_kernel, out_shape=tuple((pltpu.VMEM(shape.shape, sha...  64.1 us

profile of v6, /device:TPU:1, one launch (start us, length us, event | category | flops | bytes accessed | tf_op | source)
XLA Modules:
  0.0 66.2 jit_solution(13681860609287792995)
XLA Ops:
  1.3 64.1 %layer.1 = (bf16[1,128,1024]{2,1,0:T(8,128)(2,1)S(1)}, bf16[1,128,1024]{2,1,0:T(8,128)(2,1)S(1)}, f32[16,1024]{1,0:T(8,128)S(1)}) custom-call(s32[1,1]{1,0:T(1,128)S(6)} %copy.10.mask_hbm, s32[1,1,7]{2,1,0:T(1,128)} %lengths_hbm.1, bf16[1,128,1024]{2,1,0:T(8,128)(2,1)} %actions_hbm.1, f32[1,1024]{1,0:T(1,128)} %bitcast.1, bf16[128,4096]{1,0:T(8,128)(2,1)} %w_in_ref.1, ...), custom_call_target="tpu_custom_call" | custom-call | tf_op jit(solution)/shard_map/layer/pallas_call | solution.py:634
  65.4 0.8 %publish.1 = (bf16[1,128,1024]{2,1,0:T(8,128)(2,1)}, bf16[1,128,1024]{2,1,0:T(8,128)(2,1)}, f32[16,1024]{1,0:T(8,128)}) custom-call(bf16[1,128,1024]{2,1,0:T(8,128)(2,1)S(1)} %get-tuple-element.6.refs_0_, bf16[1,128,1024]{2,1,0:T(8,128)(2,1)S(1)} %get-tuple-element.7.refs_1_, f32[16,1024]{1,0:T(8,128)S(1)} %get-tuple-element.8.refs_2_), custom_call_target="tpu_custom_call" | custom-call | tf_op jit(solution)/shard_map/publish/pallas_call | solution.py:682

commit v7 on v6

--- a/solution.py
+++ b/solution.py
@@ -282,7 +282,7 @@
     active, slopes, weights, score_slopes, attended, normed_out, inverse_out, mixed,
     far_normed, far_active, grad_att, grad_mix, grad_hidden,
     held, landed, all_mixed, total, sums, ybuf, part, zbuf, final, wide,
-    sems,
+    sems, vouch,
 ):
     dp = lax.axis_index("dp")
     fsdp = lax.axis_index("fsdp")
@@ -295,7 +295,8 @@
     in_y = [device(x, (y + d) % 4, z, c) for d in range(1, 4)]
     in_z = [device(x, y, (z + d) % NZ, c) for d in range(1, NZ)]
     ends = [device(y, i // 2, z, i % 2) for i in range(8)]
-    begins = [device(i // 2, x, z, i % 2) for i in range(8)]
+    near_z = [device(x, y, (z + d) % NZ, c) for d in (1, 2, NZ - 1, NZ - 2)]
+    across_z = device(x, y, z + 4 - 8 * (z // 4 % 2), c)
     apart = [jnp.logical_or(x != y, i != me) for i in range(8)]
 
     used = [0]
@@ -312,13 +313,8 @@
         pltpu.make_async_copy(lengths_hbm, lengths_ref, new()),
     ]
     barrier = pltpu.get_barrier_semaphore()
-    for target in [in_z[d] for d in (7, 6, 8, 5, 9, 4, 10, 3, 11, 2, 12, 1, 13, 0, 14)] + in_group + in_y:
+    for target in near_z + [across_z] + in_group + in_y:
         pl.semaphore_signal(barrier, inc=1, device_id=target, device_id_type=MESH)
-    for i in range(8):
-        @pl.when(apart[i])
-        def _():
-            pl.semaphore_signal(barrier, inc=1, device_id=ends[i], device_id_type=MESH)
-            pl.semaphore_signal(barrier, inc=1, device_id=begins[i], device_id_type=MESH)
     start_all(loads)
 
     sections = {
@@ -340,7 +336,7 @@
     swap_send = new()
     swaps = [Swap(held.at[i], landed.at[i], at, orders[i], mask_ref, swap_send, new) for i in range(4)]
 
-    pl.semaphore_wait(barrier, 41 - 2 * (x == y).astype(jnp.int32))
+    pl.semaphore_wait(barrier, 15)
     sections[KEYS].fetch()
     for copy in loads:
         copy.wait()
@@ -357,6 +353,10 @@
     cown.start()
     sections[KEYS].start()
     sections[QUERIES].start()
+    for target in in_y:
+        pl.semaphore_signal(vouch.at[0], inc=1, device_id=target, device_id_type=MESH)
+    for d in (2, NZ - 2):
+        pl.semaphore_signal(vouch.at[1], inc=1, device_id=device(x, y, (z + d) % NZ, c), device_id_type=MESH)
 
     for r in range(0, ROWS, CHUNK):
         n, inverse = normalize(actions[r : r + CHUNK].astype(F32))
@@ -402,6 +402,10 @@
     sections[GATES].start()
     swaps[0].turn(0)
     swaps[1].turn(1)
+    pl.semaphore_wait(vouch.at[0], 3)
+    pl.semaphore_wait(vouch.at[1], 2)
+    for d in (4, NZ - 4):
+        pl.semaphore_signal(vouch.at[2], inc=1, device_id=device(x, y, (z + d) % NZ, c), device_id_type=MESH)
     sections[KEYS].across()
     sections[GATES].spread()
     sections[QUERIES].across()
@@ -453,6 +457,7 @@
         mix = (n * active[GATES, r : r + CHUNK].astype(F32)).astype(BF16)
         for h in range(HEADS):
             mixed[h, r : r + CHUNK] = mix[:, head(h)]
+    pl.semaphore_wait(vouch.at[2], 2)
     own_rows = pl.ds(pl.multiple_of(me * ROWS, ROWS), ROWS)
     msend, mrecv, ysend, yrecv, zsend, zrecv, asend, arecv = [new() for _ in range(8)]
     spread = [remote(mixed.at[group[d]], all_mixed.at[own_rows], msend, mrecv, in_group[d]) for d in range(7)]
@@ -673,6 +678,7 @@
             pltpu.VMEM((16, 128), F32),
             pltpu.VMEM((8, 16, 128), F32),
             dma((SEMAPHORES,)),
+            pltpu.SemaphoreType.REGULAR((3,)),
         ],
         compiler_params=pltpu.CompilerParams(
             collective_id=0, has_side_effects=True, vmem_limit_bytes=56 * 1024 * 1024

time: 66.4 us -> 64.8 us (0.976)
  Pallas kernels: 65 us -> 63.4 us
    pallas_call x1, Pallas kernels: 64.1 us -> 62.6 us  [per_device(): pl.pallas_call(layer_kernel, out_shape=tuple((pltpu.VMEM(shape.shape, sha...]
where the time goes in v7:
time: 64.8 us; the launch traced here: 64.7 us
  Pallas kernels  63.4 us (98%)
  between operations  1.29 us (2%)
    pallas_call x1, Pallas kernels, per_device(): pl.pallas_call(layer_kernel, out_shape=tuple((pltpu.VMEM(shape.shape, sha...  62.6 us

profile of v7, /device:TPU:1, one launch (start us, length us, event | category | flops | bytes accessed | tf_op | source)
XLA Modules:
  0.0 64.7 jit_solution(4574182071317535492)
XLA Ops:
  1.3 62.6 %layer.1 = (bf16[1,128,1024]{2,1,0:T(8,128)(2,1)S(1)}, bf16[1,128,1024]{2,1,0:T(8,128)(2,1)S(1)}, f32[16,1024]{1,0:T(8,128)S(1)}) custom-call(s32[1,1]{1,0:T(1,128)S(6)} %copy.10.mask_hbm, s32[1,1,7]{2,1,0:T(1,128)} %lengths_hbm.1, bf16[1,128,1024]{2,1,0:T(8,128)(2,1)} %actions_hbm.1, f32[1,1024]{1,0:T(1,128)} %bitcast.1, bf16[128,4096]{1,0:T(8,128)(2,1)} %w_in_ref.1, ...), custom_call_target="tpu_custom_call" | custom-call | tf_op jit(solution)/shard_map/layer/pallas_call | solution.py:639
  63.9 0.8 %publish.1 = (bf16[1,128,1024]{2,1,0:T(8,128)(2,1)}, bf16[1,128,1024]{2,1,0:T(8,128)(2,1)}, f32[16,1024]{1,0:T(8,128)}) custom-call(bf16[1,128,1024]{2,1,0:T(8,128)(2,1)S(1)} %get-tuple-element.6.refs_0_, bf16[1,128,1024]{2,1,0:T(8,128)(2,1)S(1)} %get-tuple-element.7.refs_1_, f32[16,1024]{1,0:T(8,128)S(1)} %get-tuple-element.8.refs_2_), custom_call_target="tpu_custom_call" | custom-call | tf_op jit(solution)/shard_map/publish/pallas_call | solution.py:688

commit v8 on v6

--- a/solution.py
+++ b/solution.py
@@ -26,7 +26,7 @@
     VALUES: (128, []),
     KEYS: (0, [("x", 0, 16, 0, WIDTH), ("z", 64, 16, 0, WIDTH)]),
     QUERIES: (0, [("x", 0, 16, 0, WIDTH), ("z", 64, 16, 0, WIDTH)]),
-    GATES: (64, [("x", 64, 16, 0, HALF), ("z", 64, 16, HALF, HALF)]),
+    GATES: (64, [("x", 64, 16, 0, WIDTH)]),
     OUT: (128, []),
 }
 SEMAPHORES = 78
@@ -282,7 +282,7 @@
     active, slopes, weights, score_slopes, attended, normed_out, inverse_out, mixed,
     far_normed, far_active, grad_att, grad_mix, grad_hidden,
     held, landed, all_mixed, total, sums, ybuf, part, zbuf, final, wide,
-    sems,
+    sems, vouch,
 ):
     dp = lax.axis_index("dp")
     fsdp = lax.axis_index("fsdp")
@@ -295,7 +295,13 @@
     in_y = [device(x, (y + d) % 4, z, c) for d in range(1, 4)]
     in_z = [device(x, y, (z + d) % NZ, c) for d in range(1, NZ)]
     ends = [device(y, i // 2, z, i % 2) for i in range(8)]
-    begins = [device(i // 2, x, z, i % 2) for i in range(8)]
+    near = [device((x + d) % 4, y, z, c) for d in (1, 3)] + [device(x, (y + d) % 4, z, c) for d in (1, 3)]
+    near += [device(x, y, (z + d) % NZ, c) for d in (1, NZ - 1)] + [other]
+
+    def vouch_for(step, targets):
+        for target in targets:
+            pl.semaphore_signal(vouch.at[step], inc=1, device_id=target, device_id_type=MESH)
+
     apart = [jnp.logical_or(x != y, i != me) for i in range(8)]
 
     used = [0]
@@ -312,13 +318,8 @@
         pltpu.make_async_copy(lengths_hbm, lengths_ref, new()),
     ]
     barrier = pltpu.get_barrier_semaphore()
-    for target in [in_z[d] for d in (7, 6, 8, 5, 9, 4, 10, 3, 11, 2, 12, 1, 13, 0, 14)] + in_group + in_y:
+    for target in near:
         pl.semaphore_signal(barrier, inc=1, device_id=target, device_id_type=MESH)
-    for i in range(8):
-        @pl.when(apart[i])
-        def _():
-            pl.semaphore_signal(barrier, inc=1, device_id=ends[i], device_id_type=MESH)
-            pl.semaphore_signal(barrier, inc=1, device_id=begins[i], device_id_type=MESH)
     start_all(loads)
 
     sections = {
@@ -340,7 +341,7 @@
     swap_send = new()
     swaps = [Swap(held.at[i], landed.at[i], at, orders[i], mask_ref, swap_send, new) for i in range(4)]
 
-    pl.semaphore_wait(barrier, 41 - 2 * (x == y).astype(jnp.int32))
+    pl.semaphore_wait(barrier, len(near))
     sections[KEYS].fetch()
     for copy in loads:
         copy.wait()
@@ -348,7 +349,6 @@
     held[1, 0] = actions[FIRST + 16 : LAST]
     held[2, 0] = actions[LAST:]
     held[3, 0] = cot[LAST:]
-    swaps[0].start()
     swaps[1].start()
     sections[QUERIES].fetch()
     sections[GATES].fetch()
@@ -357,6 +357,7 @@
     cown.start()
     sections[KEYS].start()
     sections[QUERIES].start()
+    vouch_for(0, near)
 
     for r in range(0, ROWS, CHUNK):
         n, inverse = normalize(actions[r : r + CHUNK].astype(F32))
@@ -392,6 +393,11 @@
     def head(h):
         return slice(h * HEAD_DIM, (h + 1) * HEAD_DIM)
 
+    pl.semaphore_wait(vouch.at[0], len(near))
+    vouch_for(1, [device(x, y, (z + d) % NZ, c) for d in (2, NZ - 2)] + [other])
+    pl.semaphore_wait(vouch.at[1], 3)
+    swaps[0].start()
+    vouch_for(2, [device(x, y, (z + d) % NZ, c) for d in (4, NZ - 4)] + in_y)
     swaps[1].turn(0)
     sections[KEYS].pass_on()
     sections[VALUES].start()
@@ -453,6 +459,7 @@
         mix = (n * active[GATES, r : r + CHUNK].astype(F32)).astype(BF16)
         for h in range(HEADS):
             mixed[h, r : r + CHUNK] = mix[:, head(h)]
+    pl.semaphore_wait(vouch.at[2], 5)
     own_rows = pl.ds(pl.multiple_of(me * ROWS, ROWS), ROWS)
     msend, mrecv, ysend, yrecv, zsend, zrecv, asend, arecv = [new() for _ in range(8)]
     spread = [remote(mixed.at[group[d]], all_mixed.at[own_rows], msend, mrecv, in_group[d]) for d in range(7)]
@@ -673,6 +680,7 @@
             pltpu.VMEM((16, 128), F32),
             pltpu.VMEM((8, 16, 128), F32),
             dma((SEMAPHORES,)),
+            pltpu.SemaphoreType.REGULAR((3,)),
         ],
         compiler_params=pltpu.CompilerParams(
             collective_id=0, has_side_effects=True, vmem_limit_bytes=56 * 1024 * 1024

time: 66.4 us -> 64 us (0.964)
  Pallas kernels: 65 us -> 62.6 us
    pallas_call x1, Pallas kernels: 64.1 us -> 61.8 us  [per_device(): pl.pallas_call(layer_kernel, out_shape=tuple((pltpu.VMEM(shape.shape, sha...]
where the time goes in v8:
time: 64 us; the launch traced here: 63.9 us
  Pallas kernels  62.6 us (98%)
  between operations  1.29 us (2%)
    pallas_call x1, Pallas kernels, per_device(): pl.pallas_call(layer_kernel, out_shape=tuple((pltpu.VMEM(shape.shape, sha...  61.8 us

profile of v8, /device:TPU:1, one launch (start us, length us, event | category | flops | bytes accessed | tf_op | source)
XLA Modules:
  0.0 63.9 jit_solution(608285270556846035)
XLA Ops:
  1.3 61.8 %layer.1 = (bf16[1,128,1024]{2,1,0:T(8,128)(2,1)S(1)}, bf16[1,128,1024]{2,1,0:T(8,128)(2,1)S(1)}, f32[16,1024]{1,0:T(8,128)S(1)}) custom-call(s32[1,1]{1,0:T(1,128)S(6)} %copy.10.mask_hbm, s32[1,1,7]{2,1,0:T(1,128)} %lengths_hbm.1, bf16[1,128,1024]{2,1,0:T(8,128)(2,1)} %actions_hbm.1, f32[1,1024]{1,0:T(1,128)} %bitcast.1, bf16[128,4096]{1,0:T(8,128)(2,1)} %w_in_ref.1, ...), custom_call_target="tpu_custom_call" | custom-call | tf_op jit(solution)/shard_map/layer/pallas_call | solution.py:641
  63.1 0.8 %publish.1 = (bf16[1,128,1024]{2,1,0:T(8,128)(2,1)}, bf16[1,128,1024]{2,1,0:T(8,128)(2,1)}, f32[16,1024]{1,0:T(8,128)}) custom-call(bf16[1,128,1024]{2,1,0:T(8,128)(2,1)S(1)} %get-tuple-element.6.refs_0_, bf16[1,128,1024]{2,1,0:T(8,128)(2,1)S(1)} %get-tuple-element.7.refs_1_, f32[16,1024]{1,0:T(8,128)S(1)} %get-tuple-element.8.refs_2_), custom_call_target="tpu_custom_call" | custom-call | tf_op jit(solution)/shard_map/publish/pallas_call | solution.py:690

commit v9 on v8

--- a/solution.py
+++ b/solution.py
@@ -409,8 +409,8 @@
     swaps[0].turn(0)
     swaps[1].turn(1)
     sections[KEYS].across()
+    sections[QUERIES].across()
     sections[GATES].spread()
-    sections[QUERIES].across()
     sections[GATES].across()
     cring.forward()
     sections[VALUES].forward()
@@ -425,9 +425,9 @@
     swaps[1].turn(2)
     far_inputs = jnp.concatenate([held[0, 3], held[1, 3]], axis=0).astype(F32)
     normed[ROWS:] = (normalize(far_inputs)[0] * gain[...]).astype(BF16)
-    sections[VALUES].finish()
     sections[KEYS].arrived()
     project(KEYS, ROWS + MOST)
+    sections[VALUES].finish()
     sections[QUERIES].arrived()
     project(QUERIES)
     sections[GATES].collect()

time: 64 us -> 63.9 us (level)
  no operation moved by 1% of the time
where the time goes in v9:
time: 63.9 us; the launch traced here: 63.8 us
  Pallas kernels  62.5 us (98%)
  between operations  1.29 us (2%)
    pallas_call x1, Pallas kernels, per_device(): pl.pallas_call(layer_kernel, out_shape=tuple((pltpu.VMEM(shape.shape, sha...  61.7 us

profile of v9, /device:TPU:1, one launch (start us, length us, event | category | flops | bytes accessed | tf_op | source)
XLA Modules:
  0.0 63.8 jit_solution(6837439149140891872)
XLA Ops:
  1.3 61.7 %layer.1 = (bf16[1,128,1024]{2,1,0:T(8,128)(2,1)S(1)}, bf16[1,128,1024]{2,1,0:T(8,128)(2,1)S(1)}, f32[16,1024]{1,0:T(8,128)S(1)}) custom-call(s32[1,1]{1,0:T(1,128)S(6)} %copy.10.mask_hbm, s32[1,1,7]{2,1,0:T(1,128)} %lengths_hbm.1, bf16[1,128,1024]{2,1,0:T(8,128)(2,1)} %actions_hbm.1, f32[1,1024]{1,0:T(1,128)} %bitcast.1, bf16[128,4096]{1,0:T(8,128)(2,1)} %w_in_ref.1, ...), custom_call_target="tpu_custom_call" | custom-call | tf_op jit(solution)/shard_map/layer/pallas_call | solution.py:641
  62.9 0.8 %publish.1 = (bf16[1,128,1024]{2,1,0:T(8,128)(2,1)}, bf16[1,128,1024]{2,1,0:T(8,128)(2,1)}, f32[16,1024]{1,0:T(8,128)}) custom-call(bf16[1,128,1024]{2,1,0:T(8,128)(2,1)S(1)} %get-tuple-element.6.refs_0_, bf16[1,128,1024]{2,1,0:T(8,128)(2,1)S(1)} %get-tuple-element.7.refs_1_, f32[16,1024]{1,0:T(8,128)S(1)} %get-tuple-element.8.refs_2_), custom_call_target="tpu_custom_call" | custom-call | tf_op jit(solution)/shard_map/publish/pallas_call | solution.py:690
